TPU v7x, 32 devices: a whole 2x2x4 slice. The times are simulated.
32 devices in a mesh: src: 4 (over y, x), tgt: 8 (over z, core).
Axes of the slice: x: 2, y: 2, z: 4, core: 2. Of those that a mesh axis runs over, the one named last changes fastest.
Arguments:
- src_values: float32 [16, 32768], P(None, ('src', 'tgt')), may hold values from -6 to 6
- src_offset: float32 [32768], P(('src', 'tgt')), may hold values from -1 to 1
- src_box: int32 [32768], P(('src', 'tgt')), may hold values from 0 to 8191, as said below
- tgt_offset: float32 [32768], P(('src', 'tgt')), may hold values from -1 to 1
- tgt_box: int32 [32768], P(('src', 'tgt')), may hold values from 0 to 8191, as said below
- pattern: int32 [13, 8192], P(None, ('src', 'tgt')), may hold values from 0 to 3
- operators: float32 [13, 4, 2, 64, 128], replicated, may hold values from -0.5 to 0.5
Outputs:
- target_values: float32 [16, 32768], P(None, ('src', 'tgt'))
Inputs may be any that keep to these rules, and one draw needn't show every extreme that they name: `src_box`: source point p lies in a box of the block [(p // 1024) * 256, (p // 1024 + 1) * 256). `tgt_box`: target point q lies in a box of the block [(q // 1024) * 256, (q // 1024 + 1) * 256).
All inputs are finite; a program needn't handle non-finite values.
Results may differ from a plain program's by a relative error of at most 0.00016.
Values sent between devices are 32-bit elements; how exact they have to be, the bound alone decides.
No kernel may reach another device: no remote copies, remote signals or barrier semaphores. Data moves between devices by JAX's collectives and lax.ppermute only.
A program may use at most 128 MiB of HBM per device.

v0:
```python
import jax
import jax.numpy as jnp
from jax import lax
from jax.sharding import PartitionSpec as P

RANK = 64
KINDS = 4


HIGHEST = lax.Precision.HIGHEST


def partner_2(value, axis, stride):
    return lax.ppermute(value, axis, [(i, i ^ 1 << stride) for i in range(lax.axis_size(axis))])


def chebyshev(points):
    rows = [jnp.ones_like(points), points]
    for order in range(2, RANK):
        rows.append(2.0 * points * rows[-1] - rows[-2])
    return jnp.stack(rows[:RANK])


def reverse_bits(values, nbits):
    lead = values.shape[:-1]
    base = len(lead)
    split = values.reshape(lead + (2,) * nbits)
    order = tuple(range(base)) + tuple(range(base + nbits - 1, base - 1, -1))
    return split.transpose(order).reshape(lead + (2**nbits,))


def local_level(coefficients, weights, pattern_row, bit_pos):
    funcs, count = (coefficients.shape[0], coefficients.shape[2])
    outer = count >> bit_pos + 1
    inner = 1 << bit_pos
    split = coefficients.reshape(funcs, RANK, outer, 2, inner)
    stacked = jnp.concatenate([split[:, :, :, 0, :], split[:, :, :, 1, :]], axis=1)
    matrix = weights.reshape(KINDS * 2 * RANK, 2 * RANK)
    products = jnp.einsum("mr,vrgh->vmgh", matrix, stacked, precision=HIGHEST)
    products = products.reshape(funcs, KINDS, 2, RANK, outer, inner)
    kinds_row = jnp.arange(KINDS)
    selector = (
        pattern_row.reshape(outer, 2, inner)[None] == kinds_row[:, None, None, None]
    ).astype(jnp.float32)
    merged = jnp.einsum("kgch,vkcrgh->vrgch", selector, products, precision=HIGHEST)
    return merged.reshape(funcs, RANK, count)


def remote_level(own, partner, weights, pattern_row, parity):
    first = jnp.where(parity == 0, own, partner)
    second = jnp.where(parity == 0, partner, own)
    stacked = jnp.concatenate([first, second], axis=1)
    chosen = jnp.where(parity == 0, weights[:, 0], weights[:, 1]).reshape(KINDS * RANK, 2 * RANK)
    products = jnp.einsum("mr,vrp->vmp", chosen, stacked, precision=HIGHEST)
    products = products.reshape(own.shape[0], KINDS, RANK, own.shape[2])
    kinds_row = jnp.arange(KINDS, dtype=pattern_row.dtype)
    selector = (pattern_row[None, :] == kinds_row[:, None]).astype(jnp.float32)
    return jnp.einsum("kp,vkrp->vrp", selector, products, precision=HIGHEST)


def on_device(src_values, src_offset, src_box, tgt_offset, tgt_box, pattern, operators):
    funcs = src_values.shape[0]
    boxes_here = pattern.shape[1]
    tgt_bits = lax.axis_size("tgt").bit_length() - 1
    src_bits = lax.axis_size("src").bit_length() - 1
    dev_bits = tgt_bits + src_bits
    devices_count = 1 << dev_bits
    upper_count = boxes_here >> dev_bits
    local_bits = boxes_here.bit_length() - 1
    box_ids = jnp.arange(boxes_here, dtype=jnp.int32)
    basis_src = chebyshev(src_offset)
    src_hot = (jnp.remainder(src_box, boxes_here)[:, None] == box_ids[None, :]).astype(jnp.float32)
    weighted = src_values[:, None, :] * basis_src[None, :, :]
    coefficients = jnp.einsum("vrp,ps->vrs", weighted, src_hot, precision=HIGHEST)
    for level in range(local_bits):
        coefficients = local_level(coefficients, operators[level], pattern[level], level)
    for level in range(dev_bits):
        if level < tgt_bits:
            partner = partner_2(coefficients, "tgt", level)
            parity = lax.axis_index("tgt") >> level & 1
        else:
            partner = partner_2(coefficients, "src", level - tgt_bits)
            parity = lax.axis_index("src") >> level - tgt_bits & 1
        coefficients = remote_level(
            coefficients,
            partner,
            operators[local_bits + level],
            pattern[local_bits + level],
            parity,
        )
    ordered = reverse_bits(coefficients.reshape(funcs, RANK, upper_count, devices_count), dev_bits)
    arrived = lax.all_to_all(ordered, ("src", "tgt"), split_axis=3, concat_axis=3, tiled=True)
    coefficients = arrived.reshape(funcs, RANK, boxes_here)
    final = reverse_bits(coefficients, local_bits)
    final = final.reshape(funcs, RANK, devices_count, upper_count)
    final = jnp.swapaxes(final, 2, 3).reshape(funcs, RANK, boxes_here)
    tgt_hot = (jnp.remainder(tgt_box, boxes_here)[:, None] == box_ids[None, :]).astype(jnp.float32)
    gathered = jnp.einsum("vrs,ps->vrp", final, tgt_hot, precision=HIGHEST)
    basis_tgt = chebyshev(tgt_offset)
    return 0.125 * jnp.einsum("vrp,rp->vp", gathered, basis_tgt, precision=HIGHEST)


def solution(mesh):
    placed = (
        P(None, ("src", "tgt")),
        P(("src", "tgt")),
        P(("src", "tgt")),
        P(("src", "tgt")),
        P(("src", "tgt")),
        P(None, ("src", "tgt")),
        P(),
    )
    return jax.shard_map(
        on_device, mesh=mesh, in_specs=placed, out_specs=P(None, ("src", "tgt")), check_vma=False
    )
```

profile of v0, /device:TPU:0, one launch (start us, length us, event | category | flops | bytes accessed | tf_op | source)
XLA Modules:
  0.0 426.1 jit_solution(18158523968778728231)
XLA Ops:
  2.7 3.1 fusion.12
  7.3 1.8 copy-done
  9.1 1.6 fusion.91
  11.3 5.5 %convolution_bitcast_fusion.7 = f32[16,512,128,1]{1,2,0,3:T(8,128)} fusion(f32[512,128,1]{1,0,2:T(8,128)S(1)} %bitcast.509, f32[16,64,128,1]{1,2,0,3:T(8,128)S(1)} %get-tuple-element.188, f32[16,64,128,1]{1,2,0,3:T(8,128)S(1)} %get-tuple-element.189), kind=kOutput, calls=%fused_computation.29 | convolution fusion | flops 1610874880 | bytes 5505024 | tf_op jit(solution)/shard_map/mr,vrgh->vmgh/dot_general | solution.py:39
  16.8 5.3 %copy.153 = f32[16,512,128,1]{2,1,0,3:T(8,128)} copy(f32[16,512,128,1]{1,2,0,3:T(8,128)} %convolution_bitcast_fusion.7) | data formatting | bytes 8388608
  22.5 2.9 multiply_reduce_fusion.7
  25.3 1.8 copy.82
  28.6 5.1 %convolution_bitcast_fusion.6 = f32[16,512,64,2]{1,2,3,0:T(8,128)} fusion(f32[512,128,1,1]{1,0,3,2:T(8,128)S(1)} %bitcast.508, f32[16,64,64,2]{1,2,3,0:T(8,128)S(1)} %bitcast.490, f32[16,64,64,2]{1,2,3,0:T(8,128)S(1)} %bitcast.493), kind=kOutput, calls=%fused_computation.28 | convolution fusion | flops 1610874880 | bytes 5505024 | tf_op jit(solution)/shard_map/mr,vrgh->vmgh/dot_general | solution.py:39
  33.7 9.8 %reshape.115 = f32[16,4,2,64,64,2]{3,2,1,4,5,0:T(2,128)} reshape(f32[16,512,64,2]{1,2,3,0:T(8,128)} %convolution_bitcast_fusion.6) | data formatting | bytes 8388608 | tf_op jit(solution)/shard_map/reshape | solution.py:40
  43.8 3.1 copy.85
  46.9 12.9 %fusion.10 = f32[64,2,2,1,16,64]{5,3,4,2,1,0:T(1,128)S(1)} fusion(pred[4,64,2,2,1,1]{0,4,5,3,2,1:T(4,128)(4,1)S(1)} %copy.85, f32[16,4,2,64,64,2]{3,2,1,4,5,0:T(2,128)} %reshape.115), kind=kOutput, calls=%fused_computation.10 | convolution fusion | flops 12582912 | bytes 5243904 | tf_op jit(solution)/shard_map/kgch,vkcrgh->vrgch/dot_general | solution.py:45
  61.3 5.1 %convolution_bitcast_fusion.5 = f32[16,512,32,4]{1,2,3,0:T(8,128)} fusion(f32[512,128,1,1]{1,0,3,2:T(8,128)S(1)} %bitcast.507, f32[16,64,32,4]{1,2,3,0:T(8,128)S(1)} %bitcast.491, f32[16,64,32,4]{1,2,3,0:T(8,128)S(1)} %bitcast.494), kind=kOutput, calls=%fused_computation.27 | convolution fusion | flops 1610874880 | bytes 5505024 | tf_op jit(solution)/shard_map/mr,vrgh->vmgh/dot_general | solution.py:39
  66.4 9.8 %reshape.116 = f32[16,4,2,64,32,4]{3,2,1,4,5,0:T(2,128)} reshape(f32[16,512,32,4]{1,2,3,0:T(8,128)} %convolution_bitcast_fusion.5) | data formatting | bytes 8388608 | tf_op jit(solution)/shard_map/reshape | solution.py:40
  76.4 1.6 copy.89
  78.1 12.9 %fusion.8 = f32[32,2,4,1,16,64]{5,3,4,2,1,0:T(1,128)S(1)} fusion(pred[4,32,2,4,1,1]{0,4,5,3,2,1:T(4,128)(4,1)S(1)} %copy.89, f32[16,4,2,64,32,4]{3,2,1,4,5,0:T(2,128)} %reshape.116), kind=kOutput, calls=%fused_computation.8 | convolution fusion | flops 12582912 | bytes 5243904 | tf_op jit(solution)/shard_map/kgch,vkcrgh->vrgch/dot_general | solution.py:45
  91.9 5.0 %convolution_bitcast_fusion.4 = f32[16,512,16,8]{1,3,2,0:T(8,128)} fusion(f32[512,128,1,1]{1,0,3,2:T(8,128)S(1)} %bitcast.506, f32[16,64,16,8]{1,3,2,0:T(8,128)S(1)} %bitcast.492, f32[16,64,16,8]{1,3,2,0:T(8,128)S(1)} %bitcast.495), kind=kOutput, calls=%fused_computation.26 | convolution fusion | flops 1610874880 | bytes 5505024 | tf_op jit(solution)/shard_map/mr,vrgh->vmgh/dot_general | solution.py:39
  96.9 9.8 %reshape.117 = f32[16,4,2,64,16,8]{3,2,1,5,4,0:T(2,128)} reshape(f32[16,512,16,8]{1,3,2,0:T(8,128)} %convolution_bitcast_fusion.4) | data formatting | bytes 8388608 | tf_op jit(solution)/shard_map/reshape | solution.py:40
  107.2 13.1 %fusion.6 = f32[16,2,8,1,16,64]{5,3,4,2,1,0:T(1,128)S(1)} fusion(pred[4,16,2,8,1,1]{0,4,5,3,2,1:T(4,128)(4,1)S(1)} %copy.93, f32[16,4,2,64,16,8]{3,2,1,5,4,0:T(2,128)} %reshape.117), kind=kOutput, calls=%fused_computation.6 | convolution fusion | flops 12582912 | bytes 5243904 | tf_op jit(solution)/shard_map/kgch,vkcrgh->vrgch/dot_general | solution.py:45
  121.3 5.1 %convolution_bitcast_fusion.3 = f32[16,512,8,16]{1,3,2,0:T(8,128)} fusion(f32[512,128,1,1]{1,0,3,2:T(8,128)S(1)} %bitcast.505, f32[16,64,8,16]{1,3,2,0:T(8,128)S(1)} %get-tuple-element.42, f32[16,64,8,16]{1,3,2,0:T(8,128)S(1)} %get-tuple-element.41), kind=kOutput, calls=%fused_computation.25 | convolution fusion | flops 1610874880 | bytes 5505024 | tf_op jit(solution)/shard_map/mr,vrgh->vmgh/dot_general | solution.py:39
  126.4 9.8 %reshape.118 = f32[16,4,2,64,8,16]{3,2,1,5,4,0:T(2,128)} reshape(f32[16,512,8,16]{1,3,2,0:T(8,128)} %convolution_bitcast_fusion.3) | data formatting | bytes 8388608 | tf_op jit(solution)/shard_map/reshape | solution.py:40
  136.7 12.9 %fusion.4 = f32[8,2,16,1,16,64]{5,3,4,2,1,0:T(1,128)S(1)} fusion(pred[4,8,2,16,1,1]{0,4,5,3,2,1:T(4,128)(4,1)S(1)} %copy.97, f32[16,4,2,64,8,16]{3,2,1,5,4,0:T(2,128)} %reshape.118), kind=kOutput, calls=%fused_computation.4 | convolution fusion | flops 12582912 | bytes 5243904 | tf_op jit(solution)/shard_map/kgch,vkcrgh->vrgch/dot_general | solution.py:45
  150.5 5.1 %convolution_bitcast_fusion.2 = f32[16,512,4,32]{1,3,2,0:T(8,128)} fusion(f32[512,128,1,1]{1,0,3,2:T(8,128)S(1)} %bitcast.504, f32[16,64,4,32]{1,3,2,0:T(8,128)S(1)} %get-tuple-element.40, f32[16,64,4,32]{1,3,2,0:T(8,128)S(1)} %get-tuple-element.39), kind=kOutput, calls=%fused_computation.24 | convolution fusion | flops 1610874880 | bytes 5505024 | tf_op jit(solution)/shard_map/mr,vrgh->vmgh/dot_general | solution.py:39
  155.5 9.8 %reshape.119 = f32[16,4,2,64,4,32]{3,2,1,5,4,0:T(2,128)} reshape(f32[16,512,4,32]{1,3,2,0:T(8,128)} %convolution_bitcast_fusion.2) | data formatting | bytes 8388608 | tf_op jit(solution)/shard_map/reshape | solution.py:40
  165.8 12.9 %fusion.2 = f32[4,2,32,1,16,64]{5,3,4,2,1,0:T(1,128)S(1)} fusion(pred[4,4,2,32,1,1]{0,4,5,3,2,1:T(4,128)(4,1)S(1)} %copy.101, f32[16,4,2,64,4,32]{3,2,1,5,4,0:T(2,128)} %reshape.119), kind=kOutput, calls=%fused_computation.2 | convolution fusion | flops 12582912 | bytes 5243904 | tf_op jit(solution)/shard_map/kgch,vkcrgh->vrgch/dot_general | solution.py:45
  179.7 5.0 %convolution_bitcast_fusion.1 = f32[16,512,2,64]{1,3,2,0:T(8,128)} fusion(f32[512,128,1,1]{1,0,3,2:T(8,128)S(1)} %bitcast.503, f32[16,64,2,64]{1,3,2,0:T(8,128)S(1)} %get-tuple-element.38, f32[16,64,2,64]{1,3,2,0:T(8,128)S(1)} %get-tuple-element.37), kind=kOutput, calls=%fused_computation.23 | convolution fusion | flops 1610874880 | bytes 5505024 | tf_op jit(solution)/shard_map/mr,vrgh->vmgh/dot_general | solution.py:39
  184.7 9.8 %reshape.120 = f32[16,4,2,64,2,64]{3,2,1,5,4,0:T(2,128)} reshape(f32[16,512,2,64]{1,3,2,0:T(8,128)} %convolution_bitcast_fusion.1) | data formatting | bytes 8388608 | tf_op jit(solution)/shard_map/reshape | solution.py:40
  194.9 13.1 %fusion = f32[2,2,64,1,16,64]{5,3,4,2,1,0:T(1,128)S(1)} fusion(pred[4,2,2,64,1,1]{0,4,5,3,2,1:T(4,128)(4,1)S(1)} %copy.105, f32[16,4,2,64,2,64]{3,2,1,5,4,0:T(2,128)} %reshape.120), kind=kOutput, calls=%fused_computation | convolution fusion | flops 12582912 | bytes 5243904 | tf_op jit(solution)/shard_map/kgch,vkcrgh->vrgch/dot_general | solution.py:45
  208.9 5.1 %convolution_bitcast_fusion = f32[16,512,1,128]{1,3,0,2:T(8,128)} fusion(f32[512,128,1]{1,0,2:T(8,128)S(1)} %bitcast.502, f32[16,64,1,128]{1,3,0,2:T(8,128)S(1)} %get-tuple-element.36, f32[16,64,1,128]{1,3,0,2:T(8,128)S(1)} %get-tuple-element.35), kind=kOutput, calls=%fused_computation.22 | convolution fusion | flops 1610874880 | bytes 5505024 | tf_op jit(solution)/shard_map/mr,vrgh->vmgh/dot_general | solution.py:39
  214.0 5.5 %copy.154 = f32[16,512,1,128]{3,1,0,2:T(8,128)} copy(f32[16,512,1,128]{1,3,0,2:T(8,128)} %convolution_bitcast_fusion) | data formatting | bytes 8388608
  219.5 2.9 multiply_reduce_fusion.6
  224.6 2.3 collective-permute-done
  227.1 3.6 fusion.14
  231.2 3.0 collective-permute-start.1
  234.3 23.4 %collective-permute-done.1 = f32[16,64,256]{2,1,0:T(8,128)S(1)} collective-permute-done((f32[16,64,256]{2,1,0:T(8,128)S(1)}, f32[16,64,256]{2,1,0:T(8,128)S(1)}, u32[]{:S(2)}, u32[]{:S(2)}) %collective-permute-start.1) | collective-permute-done | bytes 1048608 | tf_op jit(solution)/shard_map/ppermute | solution.py:14
  257.9 3.6 fusion.18
  262.1 2.8 collective-permute-start.2
  264.9 45.3 %collective-permute-done.2 = f32[16,64,256]{2,1,0:T(8,128)S(1)} collective-permute-done((f32[16,64,256]{2,1,0:T(8,128)S(1)}, f32[16,64,256]{2,1,0:T(8,128)S(1)}, u32[]{:S(2)}, u32[]{:S(2)}) %collective-permute-start.2) | collective-permute-done | bytes 1048608 | tf_op jit(solution)/shard_map/ppermute | solution.py:14
  310.5 4.0 fusion.22
  315.0 1.4 collective-permute-start.3
  316.5 22.8 %collective-permute-done.3 = f32[16,64,256]{2,1,0:T(8,128)S(1)} collective-permute-done((f32[16,64,256]{2,1,0:T(8,128)S(1)}, f32[16,64,256]{2,1,0:T(8,128)S(1)}, u32[]{:S(2)}, u32[]{:S(2)}) %collective-permute-start.3) | collective-permute-done | bytes 1048608 | tf_op jit(solution)/shard_map/ppermute | solution.py:14
  339.5 3.6 fusion.26
  345.0 22.0 %collective-permute-done.4 = f32[16,64,256]{2,1,0:T(8,128)S(1)} collective-permute-done((f32[16,64,256]{2,1,0:T(8,128)S(1)}, f32[16,64,256]{2,1,0:T(8,128)S(1)}, u32[]{:S(2)}, u32[]{:S(2)}) %collective-permute-start.4) | collective-permute-done | bytes 1048608 | tf_op jit(solution)/shard_map/ppermute | solution.py:14
  367.2 3.6 fusion.30
  374.3 2.3 reshape.211
  376.6 7.5 %all-to-all-start = ((f32[32,1,8192]{2,1,0:T(1,128)}), f32[32,1,8192]{2,1,0:T(1,128)S(1)}, u32[]{:S(2)}, u32[]{:S(2)}) async-start(f32[32,1,8192]{2,1,0:T(1,128)} %reshape.211), calls=%async_computation | async-start | bytes 2097152 | tf_op jit(solution)/shard_map/all_to_all | solution.py:92
  384.8 26.9 %all-to-all-done = f32[32,1,8192]{2,1,0:T(1,128)S(1)} async-done(((f32[32,1,8192]{2,1,0:T(1,128)}), f32[32,1,8192]{2,1,0:T(1,128)S(1)}, u32[]{:S(2)}, u32[]{:S(2)}) %all-to-all-start) | async-done | bytes 1048608 | tf_op jit(solution)/shard_map/all_to_all | solution.py:92
  412.2 3.2 reduce.44
  418.2 7.1 %multiply_reduce_fusion = f32[1024,16]{0,1:T(8,128)S(1)} fusion(f32[16,64,256]{1,2,0:T(8,128)S(1)} %bitcast.501, f32[1024,64]{0,1:T(8,128)S(1)} %bitcast.515, s32[1024]{0:T(1024)S(1)} %add_select_fusion), kind=kOutput, calls=%fused_computation.12 | convolution fusion | flops 3223568384 | bytes 1380352 | tf_op jit(solution)/shard_map/vrs,ps->vrp/dot_general | solution.py:98
  (110 shorter events, 29.4 us)
Async XLA Ops:
  7.1 2.0 copy-start
  16.8 5.3 %copy-start.13 = (s32[13,256]{1,0:T(8,128)S(1)}, s32[13,256]{1,0:T(8,128)}, u32[]{:S(2)}) copy-start(s32[13,256]{1,0:T(8,128)} %param.12) | copy-start | bytes 39940
  27.2 1.4 copy-start.6
  59.8 1.5 copy-start.5
  91.0 1.0 copy-start.4
  120.3 1.0 copy-start.3
  149.5 1.0 copy-start.2
  178.7 1.0 copy-start.1
  219.5 5.1 %copy-start.11 = (f32[4,2,64,128]{3,2,1,0:T(8,128)S(1)}, f32[4,2,64,128]{3,2,1,0:T(8,128)}, u32[]{:S(2)}) copy-start(f32[4,2,64,128]{3,2,1,0:T(8,128)} %get-tuple-element.15) | copy-start | bytes 786436
  224.0 2.8 collective-permute-start
  230.7 3.5 copy-start.10
  231.2 26.5 %collective-permute-start.1 = (f32[16,64,256]{2,1,0:T(8,128)S(1)}, f32[16,64,256]{2,1,0:T(8,128)S(1)}, u32[]{:S(2)}, u32[]{:S(2)}) collective-permute-start(f32[16,64,256]{2,1,0:T(8,128)S(1)} %bitcast.499), channel_id=1, source_target_pairs={{0,2},{1,3},{2,0},{3,1},{4,6},{5,7},{6,4},{7,5},{8,10},{9,11},{10,... | collective-permute-start | bytes 3145736 | tf_op jit(solution)/shard_map/ppermute | solution.py:14
  261.6 3.3 copy-start.9
  262.1 48.1 %collective-permute-start.2 = (f32[16,64,256]{2,1,0:T(8,128)S(1)}, f32[16,64,256]{2,1,0:T(8,128)S(1)}, u32[]{:S(2)}, u32[]{:S(2)}) collective-permute-start(f32[16,64,256]{2,1,0:T(8,128)S(1)} %bitcast.498), channel_id=1, source_target_pairs={{0,4},{1,5},{2,6},{3,7},{4,0},{5,1},{6,2},{7,3},{8,12},{9,13},{10,... | collective-permute-start | bytes 3145736 | tf_op jit(solution)/shard_map/ppermute | solution.py:14
  314.5 1.9 copy-start.8
  315.0 24.2 %collective-permute-start.3 = (f32[16,64,256]{2,1,0:T(8,128)S(1)}, f32[16,64,256]{2,1,0:T(8,128)S(1)}, u32[]{:S(2)}, u32[]{:S(2)}) collective-permute-start(f32[16,64,256]{2,1,0:T(8,128)S(1)} %bitcast.496), channel_id=1, source_target_pairs={{0,8},{8,0},{16,24},{24,16},{1,9},{9,1},{17,25},{25,17},{2,10},{10... | collective-permute-start | bytes 3145736 | tf_op jit(solution)/shard_map/ppermute | solution.py:14
  343.1 1.8 copy-start.7
  343.7 23.3 %collective-permute-start.4 = (f32[16,64,256]{2,1,0:T(8,128)S(1)}, f32[16,64,256]{2,1,0:T(8,128)S(1)}, u32[]{:S(2)}, u32[]{:S(2)}) collective-permute-start(f32[16,64,256]{2,1,0:T(8,128)S(1)} %bitcast.497), channel_id=1, source_target_pairs={{0,16},{8,24},{16,0},{24,8},{1,17},{9,25},{17,1},{25,9},{2,18},{10... | collective-permute-start | bytes 3145736 | tf_op jit(solution)/shard_map/ppermute | solution.py:14
  374.1 10.0 %copy-start.12 = (f32[1024]{0:T(1024)S(1)}, f32[1024]{0:T(1024)}, u32[]{:S(2)}) copy-start(f32[1024]{0:T(1024)} %param.10) | copy-start | bytes 12292
  374.1 10.7 %copy-start.14 = (s32[1024]{0:T(1024)S(1)}, s32[1024]{0:T(1024)}, u32[]{:S(2)}) copy-start(s32[1024]{0:T(1024)} %param.11) | copy-start | bytes 12292
  376.6 35.1 %all-to-all-start = ((f32[32,1,8192]{2,1,0:T(1,128)}), f32[32,1,8192]{2,1,0:T(1,128)S(1)}, u32[]{:S(2)}, u32[]{:S(2)}) async-start(f32[32,1,8192]{2,1,0:T(1,128)} %reshape.211), calls=%async_computation | async-start | bytes 2097152 | tf_op jit(solution)/shard_map/all_to_all | solution.py:92
where the time goes:
time: 432 us; the launch traced here: 426 us
  matrix products  147 us (34%)
  waiting for transfers between devices  143 us (33%)
  local copies, waits for them, and re-layouts  103 us (24%)
  starting transfers between devices  16.5 us (4%)
  other arithmetic  15.6 us (4%)
    ppermute x5, waiting for transfers between devices, partner_2(): lax.ppermute(value, axis, [(i, i ^ 1 << stride) for i in range(lax.axis_s...  116 us
    dot_general x6, matrix products, local_level(): jnp.einsum('kgch,vkcrgh->vrgch', selector, products, precision=HIGHEST)  77.7 us
    reshape x6, local copies, waits for them, and re-layouts, local_level(): products = products.reshape(funcs, KINDS, 2, RANK, outer, inner)  59.1 us
    dot_general x8, matrix products, local_level(): products = jnp.einsum('mr,vrgh->vmgh', matrix, stacked, precision=HIGHEST)  40.9 us
    all_to_all x1, waiting for transfers between devices, on_device(): lax.all_to_all(ordered, ('src', 'tgt'), split_axis=3, concat_axis=3, tile...  26.9 us
    unnamed x41, local copies, waits for them, and re-layouts  19.1 us
    dot_general x5, matrix products, remote_level(): products = jnp.einsum('mr,vrp->vmp', chosen, stacked, precision=HIGHEST)  18.5 us
    ppermute x5, starting transfers between devices, partner_2(): lax.ppermute(value, axis, [(i, i ^ 1 << stride) for i in range(lax.axis_s...  9.02 us
  transfers between devices with their start and end apart: 6, of which 6 were waited for; matrix products, arithmetic and copies ran while one was open for 0% of the time, Pallas kernels for 0%

commit v1 on v0

v1 whole, which is shorter than its diff:
```python
import functools

import jax
import jax.numpy as jnp
from jax import lax
from jax.experimental import pallas as pl
from jax.experimental.pallas import tpu as pltpu
from jax.sharding import Mesh
from jax.sharding import PartitionSpec as P

RANK = 64
KINDS = 4
LANES = 128
SUB = 8
ROWS_W = KINDS * 2 * RANK
ROWS = 256
REP = 2
F32 = jnp.float32
BF16 = jnp.bfloat16
I32 = jnp.int32
NT = (((1,), (1,)), ((), ()))


def iota(shape, dim):
    return lax.broadcasted_iota(jnp.int32, shape, dim)


def reverse(x, nbits):
    out = jnp.zeros_like(x)
    for b in range(nbits):
        out = out | (((x >> b) & 1) << (nbits - 1 - b))
    return out


def reverse_int(x, nbits):
    return int(format(x, "0%db" % nbits)[::-1], 2)


def rotate_left(x, by, nbits):
    by = by % nbits
    return ((x << by) | (x >> (nbits - by))) & ((1 << nbits) - 1)


def rotate_right(x, by, nbits):
    return rotate_left(x, nbits - by % nbits, nbits)


def insert(x, bit, value):
    return ((x >> bit) << (bit + 1)) | (value << bit) | (x & ((1 << bit) - 1))


def remove(x, bit):
    return ((x >> (bit + 1)) << bit) | (x & ((1 << bit) - 1))


def split(x):
    hi = x.astype(BF16)
    return hi, (x - hi.astype(F32)).astype(BF16)


def hot(cond):
    return jnp.where(cond, 1.0, 0.0).astype(BF16)


def dot(a, b):
    return jnp.dot(a, b, preferred_element_type=F32)


def chebyshev(x, out_ref):
    n = x.shape[-1]
    x = jnp.broadcast_to(x, (SUB, n))
    rows = [jnp.ones_like(x), x]
    for _ in range(2, SUB + 1):
        rows.append(2.0 * x * rows[-1] - rows[-2])
    at = iota((SUB, n), 0)
    now, before = rows[0], rows[SUB]
    for r in range(1, SUB):
        now = jnp.where(at == r, rows[r], now)
        before = jnp.where(at == r, rows[SUB - r], before)
    twice = 2.0 * rows[SUB]
    out_ref[0:SUB, :] = now
    for b in range(1, RANK // SUB):
        now, before = twice * now - before, now
        out_ref[SUB * b : SUB * b + SUB, :] = now


def box_rows(box, bits, out_ref):
    boxes = 1 << bits
    place = rotate_right(reverse(box & (boxes - 1), bits), 1, bits)
    for s in range(box.shape[1] // LANES):
        column = jnp.broadcast_to(place[:, s * LANES : (s + 1) * LANES], (LANES, LANES)).T
        for h in range(boxes // LANES):
            out_ref[s * LANES : (s + 1) * LANES, h * LANES : (h + 1) * LANES] = hot(
                column == iota((LANES, LANES), 1) + h * LANES
            )


def from_points(vals_ref, basis, boxes_hot, state):
    funcs = vals_ref.shape[0]
    pairs = boxes_hot.shape[1] // 2
    group = 4
    for g in range(0, funcs, group):
        weighted = jnp.concatenate(
            [vals_ref[g + u : g + u + 1, :] * basis[...] for u in range(group)], axis=0
        )
        hi, lo = split(weighted)
        sums = dot(hi, boxes_hot[...]) + dot(lo, boxes_hot[...])
        for u in range(group):
            part = sums[u * RANK : (u + 1) * RANK]
            part = jnp.concatenate([part[:, :pairs], part[:, pairs:]], axis=0)
            state[pl.ds(g + u, pairs, stride=funcs), :] = part.T


def swap_halves(a, b):
    low = iota(a.shape, 1) < LANES // 2
    ra, rb = pltpu.roll(a, LANES // 2, 1), pltpu.roll(b, LANES // 2, 1)
    return jnp.where(low, a, rb), jnp.where(low, ra, b)


def woven(n0, n1, funcs):
    shape = (n0.shape[0] // funcs, funcs, LANES)
    return jnp.stack([n0.reshape(shape), n1.reshape(shape)], axis=1).reshape(2 * n0.shape[0], LANES)


def halves_of(src, pairs, funcs):
    def read(r, block):
        a = src[r * funcs : (r + block) * funcs, :]
        return a, src[(pairs // 2 + r) * funcs : (pairs // 2 + r + block) * funcs, :]

    return read


def swapped(read, funcs):
    def rows(r, block):
        return woven(*swap_halves(*read(r, block)), funcs)

    return rows


def prepare(matrix, wcat):
    def piece(m):
        at = slice(m * LANES, (m + 1) * LANES)
        hi, lo = split(matrix[at, :].T)
        wcat[0:LANES, at] = hi
        wcat[LANES : 2 * LANES, at] = lo

    return [functools.partial(piece, m) for m in range(KINDS)]


def do(work):
    for piece in work:
        piece()


def share(work, step, steps):
    each = -(-len(work) // steps)
    return work[step * each : (step + 1) * each]


def choose(prod, kind, funcs):
    rows = prod.shape[0]
    kind = jnp.broadcast_to(kind[:, None, :], (rows // funcs, funcs, LANES)).reshape(rows, LANES)
    part = [prod[:, m * LANES : (m + 1) * LANES] for m in range(KINDS)]
    return jnp.where(
        kind < 1.5, jnp.where(kind < 0.5, part[0], part[1]), jnp.where(kind < 2.5, part[2], part[3])
    )


def level(rows, work, wcat, kind_of, pairs, funcs, dst):
    block = ROWS // 2 // funcs
    steps = pairs // 2 // block
    for step in range(steps):
        r = step * block
        hi, lo = split(rows(r, block))
        weights = jnp.concatenate([wcat[0:LANES, :], wcat[...]], axis=0)
        prod = dot(jnp.concatenate([lo, hi, hi], axis=1), weights)
        dst[2 * r * funcs : 2 * (r + block) * funcs, :] = choose(prod, kind_of(2 * r, 2 * block), funcs)
        do(share(work, step, steps))


def prepare_keeping(matrix, half, wide):
    def piece(m):
        at = slice(m * LANES, (m + 1) * LANES)
        turned = matrix[at, :].T
        mine = jnp.where(iota(turned.shape, 1) // RANK == half, turned, 0.0)
        moved = pltpu.roll(mine, RANK, 1)
        for n, weights in enumerate((jnp.where(half == 0, mine, moved), jnp.where(half == 0, moved, mine))):
            hi, lo = split(weights)
            wide[3 * n * LANES : (3 * n + 1) * LANES, at] = hi
            wide[(3 * n + 1) * LANES : (3 * n + 2) * LANES, at] = hi
            wide[(3 * n + 2) * LANES : (3 * n + 3) * LANES, at] = lo

    return [functools.partial(piece, m) for m in range(KINDS)]


def keeping_level(read, work, wide, kind_of, pairs, funcs, dst):
    block = ROWS // 2 // funcs
    steps = pairs // 2 // block
    for step in range(steps):
        r = step * block
        n0, n1 = swap_halves(*read(r, block))
        (hi, lo), (hi2, lo2) = split(n0), split(n1)
        prod = dot(jnp.concatenate([hi, lo, hi, hi2, lo2, hi2], axis=1), wide[...])
        dst[r * funcs : (r + block) * funcs, :] = choose(prod, kind_of(r, block), funcs)
        do(share(work, step, steps))


def copies(pairs, sems):
    out = [pltpu.make_async_copy(src, dst, sems.at[n]) for n, (src, dst) in enumerate(pairs)]
    for copy in out:
        copy.start()
    return out


def first_levels(bits, keep, last, half, pattern_of, offset, box, vals_ref, ops_buf, ops,
                 kinds, states, wcats, wide, basis, boxes_hot):
    boxes = 1 << bits
    pairs = boxes // 2
    funcs = vals_ref.shape[0]
    box_rows(box, bits, boxes_hot)
    chebyshev(offset, basis)
    lane = iota((1, boxes), 1)
    column = iota((boxes, LANES), 0)
    side = iota((boxes, LANES), 1) // RANK

    def find_kinds(l):
        row = pattern_of(l, 1)
        if l < keep:
            place = rotate_left(reverse(lane, bits), l + 1, bits)
            bit, count = l, pairs
        else:
            row = jnp.where(((lane >> keep) & 1) == half, row, 0.0)
            place = rotate_left(reverse(lane, bits), keep + 1, bits) >> 1
            bit, count = keep - 1, pairs // 2
            if l > keep:
                place = rotate_left(reverse(remove(lane, keep), bits - 1), l, bits - 1)
                bit = l
        found = jnp.where((place >> 1) == iota((count, boxes), 0), row, 0.0).astype(BF16)
        kinds[l, 0:count, :] = dot(found, hot(((column >> bit) & 1) == side))

    def ahead(l):
        if l > last:
            return []
        kinds_piece = [functools.partial(find_kinds, l)]
        if l == keep:
            return prepare_keeping(ops_buf.at[l], half, wide) + kinds_piece
        return prepare(ops_buf.at[l], wcats[l % 2]) + kinds_piece

    from_points(vals_ref, basis, boxes_hot, states[0])
    for op in ops:
        op.wait()
    do(ahead(0))

    def kind_of(l):
        return lambda at, size: kinds[l, at : at + size, :]

    for l in range(last + 1):
        now, then = states[l % 2], states[1 - l % 2]
        after = ahead(l + 1)
        if l < keep:
            level(swapped(halves_of(now, pairs, funcs), funcs), after, wcats[l % 2], kind_of(l), pairs, funcs, then)
        elif l == keep:
            keeping_level(halves_of(now, pairs, funcs), after, wide, kind_of(l), pairs, funcs, then)
        else:
            rows = swapped(halves_of(now, pairs // 2, funcs), funcs)
            level(rows, after, wcats[l % 2], kind_of(l), pairs // 2, funcs, then)
    return states[(last + 1) % 2]


def rows_to_send(bits, dev_bits, half, last_rows):
    upper = bits - dev_bits
    keep = dev_bits - 1 - REP
    boxes = 1 << bits
    lane = iota((1, boxes), 1)
    to = remove(reverse(lane & ((1 << dev_bits) - 1), dev_bits), REP)
    to = jnp.where(((lane >> keep) & 1) == half, (to << upper) | (lane >> dev_bits), -1)
    moved = lax.dot_general(
        last_rows.astype(BF16), hot(to == iota((LANES, boxes), 0)), NT, preferred_element_type=F32
    )
    return [pltpu.roll(moved, (LANES - (e << upper)) % LANES, 1) for e in range(1 << (dev_bits - 1))]


def own_kernel(
    bits, dev_bits, vals_hbm, off_hbm, box_hbm, pat_hbm, ops_hbm, out_hbm,
    vals_ref, off_ref, box_ref, pat_ref, ops_buf, kinds, state, other, wcat, wcat2, wide, basis, boxes_hot,
    sent, sems, ops_sems,
):
    levels, boxes = pat_ref.shape
    funcs = vals_ref.shape[0]
    keep = dev_bits - 1 - REP
    half = lax.axis_index("rep")
    loads = copies([(box_hbm, box_ref), (off_hbm, off_ref), (pat_hbm, pat_ref), (vals_hbm, vals_ref)], sems)
    ops = copies([(ops_hbm.at[l], ops_buf.at[l]) for l in range(dev_bits)], ops_sems)
    for load in loads:
        load.wait()

    def pattern_of(first, count):
        return pat_ref[first : first + count, :].astype(F32)

    each = sent.shape[1] - SUB
    for e, part in enumerate(rows_to_send(bits, dev_bits, half, pattern_of(levels - SUB, SUB))):
        sent[e, each:, :] = part

    last = first_levels(
        bits, keep, dev_bits - 1, half, pattern_of, off_ref[...], box_ref[...], vals_ref, ops_buf, ops,
        kinds, (state, other), (wcat, wcat2), wide, basis, boxes_hot,
    )
    quarter = boxes // 8
    for r in range(quarter):
        pair = swap_halves(*halves_of(last, 2 * quarter, funcs)(r, 1))
        rest, low = r >> (dev_bits - 2), r & ((1 << (dev_bits - 2)) - 1)
        for c in range(2):
            sent[2 * low + c, rest * funcs : (rest + 1) * funcs, :] = pair[c]
    for out in copies([(sent, out_hbm)], sems):
        out.wait()


def partner_kernel(
    bits, dev_bits, levels, points_hbm, ops_hbm, out_hbm,
    vals_ref, rest_ref, sent, ops_buf, kinds, state, other, wcat, wcat2, wide, basis, boxes_hot,
    sems, ops_sems, out_sems,
):
    funcs = vals_ref.shape[0]
    keep = dev_bits - 1 - REP
    groups = 1 << (dev_bits - 1)
    half = lax.axis_index("rep")
    loads = copies(
        [
            (points_hbm.at[pl.ds(funcs, rest_ref.shape[0]), :], rest_ref),
            (points_hbm.at[pl.ds(0, funcs), :], vals_ref),
        ],
        sems,
    )
    ops = copies([(ops_hbm.at[l], ops_buf.at[l]) for l in range(bits)], ops_sems)
    for load in loads:
        load.wait()

    def pattern_of(first, count):
        return rest_ref[first : first + count, 0 : 1 << bits]

    each = (1 << (bits - 2)) * funcs // groups
    for e, part in enumerate(rows_to_send(bits, dev_bits, half, pattern_of(levels - SUB, SUB))):
        sent[e] = part
    outs = copies([(sent, out_hbm.at[:, pl.ds(each, SUB), :])], out_sems.at[pl.ds(groups, 1)])
    last = first_levels(
        bits, keep, bits - 1, half, pattern_of, rest_ref[levels + 1 : levels + 2, :],
        rest_ref[levels : levels + 1, :].astype(I32), vals_ref, ops_buf, ops,
        kinds, (state, other), (wcat, wcat2), wide, basis, boxes_hot,
    )
    outs += copies(
        [(last.at[pl.ds(e * each, each), :], out_hbm.at[e, pl.ds(0, each), :]) for e in range(groups)], out_sems
    )
    for out in outs:
        out.wait()


def later_kinds(bits, dev_bits, table, half, l, nbits):
    upper = bits - dev_bits
    pairs = 1 << (nbits - 1)
    row = iota((2 * pairs, LANES), 0)
    at = rotate_right(2 * (row & (pairs - 1)) + (row >> (nbits - 1)), l - dev_bits + 1, nbits)
    if nbits < bits:
        at = insert(at, dev_bits - 1 - REP, half)
    column = iota((1, table.shape[0]), 1)
    device = reverse(insert(column >> 3, REP, half), dev_bits)
    lane = iota((1, LANES), 1)
    lane_key = jnp.where(lane < (1 << upper), reverse(lane, upper), -1)
    low = jnp.concatenate([at & ((1 << dev_bits) - 1)] * (table.shape[0] // LANES), axis=1)
    wanted = jnp.where((column & (SUB - 1)) == l - dev_bits, device, -1)
    picked = dot(hot(low == wanted), table)
    picked = jnp.where((at >> dev_bits) == lane_key, picked, 0.0).astype(BF16)
    spread = hot(iota((2 * LANES, LANES), 0) // LANES == iota((2 * LANES, LANES), 1) // RANK)
    return dot(jnp.concatenate([picked[:pairs], picked[pairs:]], axis=1), spread)


def later_kernel(
    bits, dev_bits, funcs, came, ops_hbm, out_ref, weights,
    ops_buf, own_kinds, state, other, wcat, wcat2, ops_sems,
):
    groups = 1 << (dev_bits - 1)
    pairs = 1 << (bits - 2)
    count = bits + REP - dev_bits
    half = lax.axis_index("rep")
    ops = copies([(ops_hbm.at[dev_bits + n], ops_buf.at[n]) for n in range(bits)], ops_sems)
    each = came.shape[1] - SUB
    table = came[:, each:, :].reshape(groups * SUB, LANES).astype(BF16)
    for n in range(count):
        own_kinds[n] = later_kinds(bits, dev_bits, table, half, dev_bits + n, bits - 1)
    for op in ops:
        op.wait()

    def arrived(r, block):
        parts = []
        for j in range(2 * r, 2 * r + 2 * block):
            g, rest = reverse_int(j & (groups - 1), dev_bits - 1), j >> (dev_bits - 1)
            parts.append(came[g, rest * funcs : (rest + 1) * funcs, :])
        return jnp.concatenate(parts, axis=0)

    states, wcats = (state, other), (wcat, wcat2)

    def ahead(n):
        return prepare(ops_buf.at[n], wcats[n % 2]) if n < count else []

    do(ahead(0))
    for n in range(count):
        now, then = states[n % 2], out_ref.at[pl.ds(0, pairs * funcs), :] if n == count - 1 else states[1 - n % 2]
        rows = arrived if n == 0 else swapped(halves_of(now, pairs, funcs), funcs)
        level(
            rows, ahead(n + 1), wcats[n % 2], lambda at, size, n=n: own_kinds[n, at : at + size, :],
            pairs, funcs, then,
        )
    for n in range(dev_bits):
        do(prepare(ops_buf.at[bits - dev_bits + n], weights.at[n]))
        if n >= REP:
            at = pairs * funcs + 2 * pairs * (n - REP)
            out_ref[at : at + 2 * pairs, :] = later_kinds(bits, dev_bits, table, half, bits + n, bits)


def join_kernel(
    bits, dev_bits, came, own, weights, off_ref, box_ref, out_ref,
    kinds, state, other, basis, final,
):
    funcs, npts = out_ref.shape
    boxes = 1 << bits
    pairs = boxes // 2
    groups = 1 << (dev_bits - 1)
    slot = came.shape[1] - SUB
    each = slot // funcs
    half = lax.axis_index("rep")
    chebyshev(off_ref[...], basis)

    def arrived(r, block):
        def rows(first):
            parts = [came[reverse_int(g, dev_bits - 1), 0:slot, :] for g in range(first // each, (first + block) // each)]
            return jnp.concatenate(parts, axis=0)

        return rows(r), rows(pairs // 4 + r)

    table = came[:, slot:, :].reshape(-1, LANES).astype(BF16)

    def find_kinds(n):
        if n < REP:
            kinds[n, 0 : pairs // 2, :] = later_kinds(bits, dev_bits, table, 1 - half, bits + n, bits - 1)
        else:
            at = pairs // 2 * funcs + pairs * (n - REP)
            kinds[n] = own[at : at + pairs, :] + later_kinds(bits, dev_bits, table, 1 - half, bits + n, bits)

    find_kinds(0)

    def kind_of(n, at, size):
        return kinds[n, at : at + size, :]

    states = (state, other)
    for n in range(dev_bits):
        now, then = states[n % 2], states[1 - n % 2]
        count = pairs // 2 if n < REP else pairs
        work = [functools.partial(find_kinds, n + 1)] if n + 1 < dev_bits else []
        read = arrived if n == 0 else halves_of(now, count, funcs)
        if n == REP:

            def read(r, block, now=now):
                a, b = (ref[r * funcs : (r + block) * funcs, :] for ref in (own, now))
                return jnp.where(half == 0, a, b), jnp.where(half == 0, b, a)

        level(
            swapped(read, funcs), work, weights.at[n], functools.partial(kind_of, n),
            count, funcs, then,
        )
    last = states[dev_bits % 2]

    for v in range(funcs):
        turned = last[pl.ds(v, pairs, stride=funcs), :].T
        hi, lo = split(turned)
        final[v * RANK : (v + 1) * RANK, :] = jnp.concatenate([hi[:RANK], hi[RANK:], lo[:RANK], lo[RANK:]], axis=1)
    width = 256
    for s in range(npts // width):
        cut = slice(s * width, (s + 1) * width)
        row = iota((boxes, width), 0)
        one = hot(2 * (row & (pairs - 1)) + (row >> (bits - 1)) == (box_ref[:, cut] & (boxes - 1)))
        found = dot(final[...], jnp.concatenate([one, one], axis=0))
        found = found.reshape(funcs, RANK, width) * basis[:, cut][None]
        out_ref[:, cut] = 0.125 * jnp.sum(found, axis=1)


VMEM = pl.BlockSpec(memory_space=pltpu.VMEM)
HBM = pl.BlockSpec(memory_space=pltpu.HBM)
DMA = pltpu.SemaphoreType.DMA


def cost(levels, rows):
    return pl.CostEstimate(flops=int(levels * rows * 2 * 512 * 512), bytes_accessed=4 << 20, transcendentals=0)


def on_device(axes, src_values, src_offset, src_box, tgt_offset, tgt_box, pattern, operators):
    funcs, npts = src_values.shape
    levels, boxes = pattern.shape
    bits = boxes.bit_length() - 1
    dev_bits = levels - bits
    groups = 1 << (dev_bits - 1)
    pairs = boxes // 2
    rows = pairs * funcs
    each = rows // 2 // groups
    ops = operators.reshape(levels, ROWS_W, 2 * RANK)
    exchange = tuple(axis for axis in axes if axis != "rep")

    def theirs(x):
        return lax.ppermute(x, "rep", [(0, 1), (1, 0)])

    def flat(x):
        return x.reshape(1, npts)

    def array(shape, dtype=F32):
        return jax.ShapeDtypeStruct(shape, dtype)

    def call(kernel, name, levels_done, arrays, out, scratch, out_specs, in_place=False):
        return pl.pallas_call(
            functools.partial(kernel, bits, dev_bits),
            out_shape=out,
            in_specs=[VMEM if in_place and x is not ops else HBM for x in arrays],
            out_specs=out_specs,
            scratch_shapes=scratch,
            compiler_params=pltpu.CompilerParams(vmem_limit_bytes=(32 if in_place else 60) << 20),
            cost_estimate=cost(levels_done, rows),
            name=name,
        )(*arrays)

    points = [
        pltpu.VMEM((funcs, npts), F32),
        pltpu.VMEM((1, npts), F32),
        pltpu.VMEM((1, npts), I32),
        pltpu.VMEM((levels, boxes), I32),
    ]
    states = [pltpu.VMEM((rows, LANES), F32)] * 2
    weights = [pltpu.VMEM((2 * LANES, ROWS_W), BF16)] * 2
    wide = [pltpu.VMEM((6 * LANES, ROWS_W), BF16)]
    sources = [pltpu.VMEM((RANK, npts), F32), pltpu.VMEM((npts, boxes), BF16)]

    def operators_of(count):
        return [pltpu.VMEM((count, ROWS_W, LANES), F32)]

    def kinds_of(count, kind_pairs=pairs):
        return [pltpu.VMEM((count, kind_pairs, LANES), F32)]

    rest = (levels + 2 + SUB - 1) // SUB * SUB
    row = iota((funcs + rest, npts), 0)
    packed = jnp.pad(pattern, ((funcs, rest - levels), (0, npts - boxes)))
    packed = jnp.where(row == funcs + levels, src_box[None], packed).astype(F32)
    packed = jnp.where(row > funcs + levels, src_offset[None], packed)
    packed = jnp.where(row < funcs, jnp.pad(src_values, ((0, rest), (0, 0))), packed)
    others = theirs(packed)

    sent = call(
        own_kernel, "own_half", dev_bits,
        (src_values, flat(src_offset), flat(src_box), pattern, ops),
        array((groups, each + SUB, LANES)),
        points + operators_of(dev_bits) + kinds_of(dev_bits) + states + weights + wide + sources
        + [pltpu.VMEM((groups, each + SUB, LANES), F32), DMA((4,)), DMA((dev_bits,))],
        HBM,
    )
    sent, others = lax.optimization_barrier((sent, others))
    arrived = lax.all_to_all(sent, exchange, split_axis=0, concat_axis=0, tiled=True)
    sent = call(
        lambda bits, dev_bits, *refs: partner_kernel(bits, dev_bits, levels, *refs), "partner_half", bits,
        (others, ops),
        array((groups, each + SUB, LANES)),
        [points[0], pltpu.VMEM((rest, npts), F32), pltpu.VMEM((groups, SUB, LANES), F32)]
        + operators_of(bits) + kinds_of(bits) + states + weights + wide + sources
        + [DMA((2,)), DMA((bits,)), DMA((groups + 1,))],
        HBM,
    )
    other_arrived = lax.all_to_all(sent, exchange, split_axis=0, concat_axis=0, tiled=True)
    count = bits + REP - dev_bits
    own, later_weights = call(
        lambda bits, dev_bits, *refs: later_kernel(bits, dev_bits, funcs, *refs), "own_later", count // 2 + 1,
        (arrived, ops),
        (
            array((rows // 2 + (dev_bits - REP) * pairs, LANES)),
            array((dev_bits, 2 * LANES, ROWS_W), BF16),
        ),
        operators_of(bits) + kinds_of(count, pairs // 2) + [pltpu.VMEM((rows // 2, LANES), F32)] * 2
        + weights + [DMA((bits,))],
        (VMEM, VMEM),
        True,
    )
    return call(
        join_kernel, "join", dev_bits,
        (other_arrived, own, later_weights, flat(tgt_offset), flat(tgt_box)),
        array((funcs, npts)),
        kinds_of(dev_bits) + states + [pltpu.VMEM((RANK, npts), F32), pltpu.VMEM((funcs * RANK, 2 * boxes), BF16)],
        VMEM,
        True,
    )


def solution(mesh):
    src, tgt = mesh.shape["src"], mesh.shape["tgt"]
    axes = ("src", "far", "rep", "near")
    devices = mesh.devices.reshape(src, tgt >> (REP + 1), 2, 1 << REP)
    placed = (P(None, axes), P(axes), P(axes), P(axes), P(axes), P(None, axes), P())
    return jax.shard_map(
        functools.partial(on_device, axes),
        mesh=Mesh(devices, axes),
        in_specs=placed,
        out_specs=P(None, axes),
        check_vma=False,
    )
```

time: 432 us -> 53 us (0.12); the launches traced: 426 us -> 52.6 us
  matrix products: 147 us -> 0 us
  waiting for transfers between devices: 143 us -> 5.48 us
  local copies, waits for them, and re-layouts: 103 us -> 1.97 us
  Pallas kernels: 0 us -> 30.5 us
  other arithmetic: 15.6 us -> 0.94 us
    dot_general x21 -> x0, matrix products: 147 us -> none  [the longest x6 77.7 us: local_level(): jnp.einsum('kgch,vkcrgh->vrgch', selector, products, precision=HIGHEST)]
    ppermute x5 -> x1, waiting for transfers between devices: 116 us -> 0.01 us  [theirs(): return lax.ppermute(x, 'rep', [(0, 1), (1, 0)])]
    reshape x8 -> x0, local copies, waits for them, and re-layouts: 60.2 us -> none  [the longest x6 59.1 us: local_level(): products = products.reshape(funcs, KINDS, 2, RANK, outer, inner)]
    pallas_call x0 -> x4, Pallas kernels: none -> 30.5 us  [call(): pl.pallas_call(functools.partial(kernel, bits, dev_bits), out_shape=out,...]
    all_to_all x1 -> x2, waiting for transfers between devices: 26.9 us -> 5.48 us  [on_device(): lax.all_to_all(sent, exchange, split_axis=0, concat_axis=0, tiled=True)]
    unnamed x41 -> x8, local copies, waits for them, and re-layouts: 19.1 us -> 1.97 us
    dot_general x8 -> x0, local copies, waits for them, and re-layouts: 7.88 us -> none  [the longest x6 5.3 us: local_level(): jnp.einsum('kgch,vkcrgh->vrgch', selector, products, precision=HIGHEST)]
    eq x13 -> x0, local copies, waits for them, and re-layouts: 6.67 us -> none  [local_level(): pattern_row.reshape(outer, 2, inner)[None] == kinds_row[:, None, None, None]]
  transfers between devices with their start and end apart: 6 -> 3, of which waited for: 6 -> 2; matrix products, arithmetic and copies ran while one was open for 0% -> 0% of each run, Pallas kernels for 0% -> 45%
where the time goes in v1:
time: 53 us; the launch traced here: 52.6 us
  Pallas kernels  30.5 us (58%)
  starting transfers between devices  13.6 us (26%)
  waiting for transfers between devices  5.48 us (10%)
  local copies, waits for them, and re-layouts  1.97 us (4%)
  other arithmetic  0.94 us (2%)
    pallas_call x4, Pallas kernels, call(): pl.pallas_call(functools.partial(kernel, bits, dev_bits), out_shape=out,...  30.5 us
    all_to_all x2, starting transfers between devices, on_device(): lax.all_to_all(sent, exchange, split_axis=0, concat_axis=0, tiled=True)  9.51 us
    all_to_all x2, waiting for transfers between devices, on_device(): lax.all_to_all(sent, exchange, split_axis=0, concat_axis=0, tiled=True)  5.48 us
    ppermute x1, starting transfers between devices, theirs(): return lax.ppermute(x, 'rep', [(0, 1), (1, 0)])  4.11 us
    unnamed x8, local copies, waits for them, and re-layouts  1.97 us
  transfers between devices with their start and end apart: 3, of which 2 were waited for; matrix products, arithmetic and copies ran while one was open for 0% of the time, Pallas kernels for 45%

profile of v1, /device:TPU:0, one launch (start us, length us, event | category | flops | bytes accessed | tf_op | source)
XLA Modules:
  0.0 52.6 jit_solution(14059560699209253975)
XLA Ops:
  0.0 0.9 %select_select_fusion = f32[32,1024]{1,0:T(8,128)S(1)} fusion(s32[13,256]{1,0:T(8,128)} %pat_hbm.1, f32[16,1024]{1,0:T(8,128)} %vals_hbm.1, s32[1024]{0:T(1024)} %param.9, f32[1024]{0:T(1024)} %param.8, pred[32]{0:T(512)(128)(4,1)S(1)} %get-tuple-element.13, pred[32]{0:T(512)(128)(4,1)S(1)} %get-tuple-element.14, pred[32]{0:T(512)(128)(4,1)S(1)} %iota_compare_fusion.2), kind=kLoop, calls=%fused_computation | loop fusion | flops 131072 | bytes 218208 | tf_op jit(solution)/shard_map/jit(_where)/select_n | solution.py:549
  0.9 4.1 %collective-permute-start = (f32[32,1024]{1,0:T(8,128)S(1)}, f32[32,1024]{1,0:T(8,128)S(1)}, u32[]{:S(2)}, u32[]{:S(2)}) collective-permute-start(f32[32,1024]{1,0:T(8,128)S(1)} %select_select_fusion), channel_id=1, source_target_pairs={{0,4},{4,0},{1,5},{5,1},{2,6},{6,2},{3,7},{7,3},{8,12},{12,8},{9,1... | collective-permute-start | bytes 393224 | tf_op jit(solution)/shard_map/ppermute | solution.py:507
  5.1 8.5 %own_half.1 = f32[16,72,128]{2,1,0:T(8,128)} custom-call(f32[16,1024]{1,0:T(8,128)} %vals_hbm.1, f32[1,1024]{1,0:T(1,128)} %bitcast.11, s32[1,1024]{1,0:T(1,128)} %bitcast.10, s32[13,256]{1,0:T(8,128)} %pat_hbm.1, f32[13,512,128]{2,1,0:T(8,128)} %bitcast.5), custom_call_target="tpu_custom_call" | custom-call | flops 5368709120 | bytes 4194304 | tf_op jit(solution)/shard_map/own_half/pallas_call | solution.py:516
  13.6 0.0 collective-permute-done.refs_0_
  13.6 0.0 copy-start.3
  13.6 4.9 %all-to-all-start.1 = ((f32[16,72,128]{2,1,0:T(8,128)}), f32[16,72,128]{2,1,0:T(8,128)S(1)}, u32[]{:S(2)}, u32[]{:S(2)}) async-start(f32[16,72,128]{2,1,0:T(8,128)} %own_half.1), calls=%async_computation.1 | async-start | bytes 1179648 | tf_op jit(solution)/shard_map/all_to_all | solution.py:561
  18.5 0.0 copy-done.3
  18.5 10.7 %partner_half.1 = f32[16,72,128]{2,1,0:T(8,128)} custom-call(f32[32,1024]{1,0:T(8,128)} %copy-done.3, f32[13,512,128]{2,1,0:T(8,128)} %bitcast.6), custom_call_target="tpu_custom_call" | custom-call | flops 8589934592 | bytes 4194304 | tf_op jit(solution)/shard_map/partner_half/pallas_call | solution.py:516
  29.2 0.5 all-to-all-done.1.refs_0_
  29.7 4.6 %all-to-all-start = ((f32[16,72,128]{2,1,0:T(8,128)}), f32[16,72,128]{2,1,0:T(8,128)S(1)}, u32[]{:S(2)}, u32[]{:S(2)}) async-start(f32[16,72,128]{2,1,0:T(8,128)} %partner_half.1), calls=%async_computation | async-start | bytes 1179648 | tf_op jit(solution)/shard_map/all_to_all | solution.py:571
  34.4 0.0 copy-start
  34.4 2.0 %copy-done = f32[13,4,2,64,128]{4,3,2,1,0:T(8,128)S(1)} copy-done((f32[13,4,2,64,128]{4,3,2,1,0:T(8,128)S(1)}, f32[13,4,2,64,128]{4,3,2,1,0:T(8,128)}, u32[]{:S(2)}) %copy-start) | copy-done | bytes 3407896
  36.3 0.0 copy-start.1
  36.3 0.0 copy-start.2
  36.3 4.3 %own_later.1 = (f32[1408,128]{1,0:T(8,128)S(1)}, bf16[5,256,512]{2,1,0:T(8,128)(2,1)S(1)}) custom-call(f32[16,72,128]{2,1,0:T(8,128)S(1)} %all-to-all-done.1.refs_0_, f32[13,512,128]{2,1,0:T(8,128)S(1)} %bitcast.7), custom_call_target="tpu_custom_call" | custom-call | flops 3221225472 | bytes 4194304 | tf_op jit(solution)/shard_map/own_later/pallas_call | solution.py:516
  40.6 5.0 %all-to-all-done.came = f32[16,72,128]{2,1,0:T(8,128)S(1)} async-done(((f32[16,72,128]{2,1,0:T(8,128)}), f32[16,72,128]{2,1,0:T(8,128)S(1)}, u32[]{:S(2)}, u32[]{:S(2)}) %all-to-all-start) | async-done | bytes 589856 | tf_op jit(solution)/shard_map/all_to_all | solution.py:571
  45.6 0.0 copy-done.1
  45.6 0.0 copy-done.2
  45.6 6.9 %join.1 = f32[16,1024]{1,0:T(8,128)} custom-call(f32[16,72,128]{2,1,0:T(8,128)S(1)} %all-to-all-done.came, f32[1408,128]{1,0:T(8,128)S(1)} %get-tuple-element.11.own, bf16[5,256,512]{2,1,0:T(8,128)(2,1)S(1)} %get-tuple-element.12.weights, f32[1,1024]{1,0:T(1,128)S(1)} %bitcast.8, s32[1,1024]{1,0:T(1,128)S(1)} %bitcast.9), custom_call_target="tpu_custom_call" | custom-call | flops 5368709120 | bytes 4194304 | tf_op jit(solution)/shard_map/join/pallas_call | solution.py:516
  (2 shorter events, 0.0 us)
Async XLA Ops:
  0.9 12.6 %collective-permute-start = (f32[32,1024]{1,0:T(8,128)S(1)}, f32[32,1024]{1,0:T(8,128)S(1)}, u32[]{:S(2)}, u32[]{:S(2)}) collective-permute-start(f32[32,1024]{1,0:T(8,128)S(1)} %select_select_fusion), channel_id=1, source_target_pairs={{0,4},{4,0},{1,5},{5,1},{2,6},{6,2},{3,7},{7,3},{8,12},{12,8},{9,1... | collective-permute-start | bytes 393224 | tf_op jit(solution)/shard_map/ppermute | solution.py:507
  13.6 4.9 %copy-start.3 = (f32[32,1024]{1,0:T(8,128)}, f32[32,1024]{1,0:T(8,128)S(1)}, u32[]{:S(2)}) copy-start(f32[32,1024]{1,0:T(8,128)S(1)} %collective-permute-done.refs_0_) | copy-start | bytes 393220
  13.6 16.1 %all-to-all-start.1 = ((f32[16,72,128]{2,1,0:T(8,128)}), f32[16,72,128]{2,1,0:T(8,128)S(1)}, u32[]{:S(2)}, u32[]{:S(2)}) async-start(f32[16,72,128]{2,1,0:T(8,128)} %own_half.1), calls=%async_computation.1 | async-start | bytes 1179648 | tf_op jit(solution)/shard_map/all_to_all | solution.py:561
  29.7 15.9 %all-to-all-start = ((f32[16,72,128]{2,1,0:T(8,128)}), f32[16,72,128]{2,1,0:T(8,128)S(1)}, u32[]{:S(2)}, u32[]{:S(2)}) async-start(f32[16,72,128]{2,1,0:T(8,128)} %partner_half.1), calls=%async_computation | async-start | bytes 1179648 | tf_op jit(solution)/shard_map/all_to_all | solution.py:571
  34.4 2.0 %copy-start = (f32[13,4,2,64,128]{4,3,2,1,0:T(8,128)S(1)}, f32[13,4,2,64,128]{4,3,2,1,0:T(8,128)}, u32[]{:S(2)}) copy-start(f32[13,4,2,64,128]{4,3,2,1,0:T(8,128)} %param.13) | copy-start | bytes 10223620
  36.3 9.3 %copy-start.1 = (f32[1024]{0:T(1024)S(1)}, f32[1024]{0:T(1024)}, u32[]{:S(2)}) copy-start(f32[1024]{0:T(1024)} %param.10) | copy-start | bytes 12292
  36.3 9.3 %copy-start.2 = (s32[1024]{0:T(1024)S(1)}, s32[1024]{0:T(1024)}, u32[]{:S(2)}) copy-start(s32[1024]{0:T(1024)} %param.11) | copy-start | bytes 12292

commit v2 on v1

--- a/solution.py
+++ b/solution.py
@@ -47,6 +47,10 @@
 
 def insert(x, bit, value):
     return ((x >> bit) << (bit + 1)) | (value << bit) | (x & ((1 << bit) - 1))
+
+
+def slot(group, dev_bits):
+    return rotate_right(group, REP, dev_bits - 1)
 
 
 def remove(x, bit):
@@ -86,7 +90,7 @@
 
 def box_rows(box, bits, out_ref):
     boxes = 1 << bits
-    place = rotate_right(reverse(box & (boxes - 1), bits), 1, bits)
+    place = reverse(box & (boxes - 1), bits)
     for s in range(box.shape[1] // LANES):
         column = jnp.broadcast_to(place[:, s * LANES : (s + 1) * LANES], (LANES, LANES)).T
         for h in range(boxes // LANES):
@@ -212,7 +216,7 @@
     return out
 
 
-def first_levels(bits, keep, last, half, pattern_of, offset, box, vals_ref, ops_buf, ops,
+def first_levels(bits, keep, last, half, pattern_of, offset, box, vals_ref, ops_buf,
                  kinds, states, wcats, wide, basis, boxes_hot):
     boxes = 1 << bits
     pairs = boxes // 2
@@ -246,19 +250,21 @@
             return prepare_keeping(ops_buf.at[l], half, wide) + kinds_piece
         return prepare(ops_buf.at[l], wcats[l % 2]) + kinds_piece
 
+    do(ahead(0))
     from_points(vals_ref, basis, boxes_hot, states[0])
-    for op in ops:
-        op.wait()
-    do(ahead(0))
 
     def kind_of(l):
         return lambda at, size: kinds[l, at : at + size, :]
+
+    def paired_already(r, block):
+        return states[0][2 * r * funcs : 2 * (r + block) * funcs, :]
 
     for l in range(last + 1):
         now, then = states[l % 2], states[1 - l % 2]
         after = ahead(l + 1)
         if l < keep:
-            level(swapped(halves_of(now, pairs, funcs), funcs), after, wcats[l % 2], kind_of(l), pairs, funcs, then)
+            rows = swapped(halves_of(now, pairs, funcs), funcs) if l > 0 else paired_already
+            level(rows, after, wcats[l % 2], kind_of(l), pairs, funcs, then)
         elif l == keep:
             keeping_level(halves_of(now, pairs, funcs), after, wide, kind_of(l), pairs, funcs, then)
         else:
@@ -291,7 +297,7 @@
     half = lax.axis_index("rep")
     loads = copies([(box_hbm, box_ref), (off_hbm, off_ref), (pat_hbm, pat_ref), (vals_hbm, vals_ref)], sems)
     ops = copies([(ops_hbm.at[l], ops_buf.at[l]) for l in range(dev_bits)], ops_sems)
-    for load in loads:
+    for load in loads + ops:
         load.wait()
 
     def pattern_of(first, count):
@@ -299,10 +305,10 @@
 
     each = sent.shape[1] - SUB
     for e, part in enumerate(rows_to_send(bits, dev_bits, half, pattern_of(levels - SUB, SUB))):
-        sent[e, each:, :] = part
+        sent[slot(e, dev_bits), each:, :] = part
 
     last = first_levels(
-        bits, keep, dev_bits - 1, half, pattern_of, off_ref[...], box_ref[...], vals_ref, ops_buf, ops,
+        bits, keep, dev_bits - 1, half, pattern_of, off_ref[...], box_ref[...], vals_ref, ops_buf,
         kinds, (state, other), (wcat, wcat2), wide, basis, boxes_hot,
     )
     quarter = boxes // 8
@@ -310,7 +316,7 @@
         pair = swap_halves(*halves_of(last, 2 * quarter, funcs)(r, 1))
         rest, low = r >> (dev_bits - 2), r & ((1 << (dev_bits - 2)) - 1)
         for c in range(2):
-            sent[2 * low + c, rest * funcs : (rest + 1) * funcs, :] = pair[c]
+            sent[slot(2 * low + c, dev_bits), rest * funcs : (rest + 1) * funcs, :] = pair[c]
     for out in copies([(sent, out_hbm)], sems):
         out.wait()
 
@@ -332,7 +338,7 @@
         sems,
     )
     ops = copies([(ops_hbm.at[l], ops_buf.at[l]) for l in range(bits)], ops_sems)
-    for load in loads:
+    for load in loads + ops:
         load.wait()
 
     def pattern_of(first, count):
@@ -340,15 +346,15 @@
 
     each = (1 << (bits - 2)) * funcs // groups
     for e, part in enumerate(rows_to_send(bits, dev_bits, half, pattern_of(levels - SUB, SUB))):
-        sent[e] = part
-    outs = copies([(sent, out_hbm.at[:, pl.ds(each, SUB), :])], out_sems.at[pl.ds(groups, 1)])
+        sent[slot(e, dev_bits)] = part
     last = first_levels(
         bits, keep, bits - 1, half, pattern_of, rest_ref[levels + 1 : levels + 2, :],
-        rest_ref[levels : levels + 1, :].astype(I32), vals_ref, ops_buf, ops,
+        rest_ref[levels : levels + 1, :].astype(I32), vals_ref, ops_buf,
         kinds, (state, other), (wcat, wcat2), wide, basis, boxes_hot,
     )
+    outs = copies([(sent, out_hbm.at[:, pl.ds(each, SUB), :])], out_sems.at[pl.ds(groups, 1)])
     outs += copies(
-        [(last.at[pl.ds(e * each, each), :], out_hbm.at[e, pl.ds(0, each), :]) for e in range(groups)], out_sems
+        [(last.at[pl.ds(e * each, each), :], out_hbm.at[slot(e, dev_bits), pl.ds(0, each), :]) for e in range(groups)], out_sems
     )
     for out in outs:
         out.wait()
@@ -362,7 +368,7 @@
     if nbits < bits:
         at = insert(at, dev_bits - 1 - REP, half)
     column = iota((1, table.shape[0]), 1)
-    device = reverse(insert(column >> 3, REP, half), dev_bits)
+    device = reverse(insert(rotate_left(column >> 3, REP, dev_bits - 1), REP, half), dev_bits)
     lane = iota((1, LANES), 1)
     lane_key = jnp.where(lane < (1 << upper), reverse(lane, upper), -1)
     low = jnp.concatenate([at & ((1 << dev_bits) - 1)] * (table.shape[0] // LANES), axis=1)
@@ -393,7 +399,7 @@
         parts = []
         for j in range(2 * r, 2 * r + 2 * block):
             g, rest = reverse_int(j & (groups - 1), dev_bits - 1), j >> (dev_bits - 1)
-            parts.append(came[g, rest * funcs : (rest + 1) * funcs, :])
+            parts.append(came[slot(g, dev_bits), rest * funcs : (rest + 1) * funcs, :])
         return jnp.concatenate(parts, axis=0)
 
     states, wcats = (state, other), (wcat, wcat2)
@@ -424,19 +430,19 @@
     boxes = 1 << bits
     pairs = boxes // 2
     groups = 1 << (dev_bits - 1)
-    slot = came.shape[1] - SUB
-    each = slot // funcs
+    size = came.shape[1] - SUB
+    each = size // funcs
     half = lax.axis_index("rep")
     chebyshev(off_ref[...], basis)
 
     def arrived(r, block):
         def rows(first):
-            parts = [came[reverse_int(g, dev_bits - 1), 0:slot, :] for g in range(first // each, (first + block) // each)]
+            parts = [came[slot(reverse_int(g, dev_bits - 1), dev_bits), 0:size, :] for g in range(first // each, (first + block) // each)]
             return jnp.concatenate(parts, axis=0)
 
         return rows(r), rows(pairs // 4 + r)
 
-    table = came[:, slot:, :].reshape(-1, LANES).astype(BF16)
+    table = came[:, size:, :].reshape(-1, LANES).astype(BF16)
 
     def find_kinds(n):
         if n < REP:
@@ -501,7 +507,7 @@
     rows = pairs * funcs
     each = rows // 2 // groups
     ops = operators.reshape(levels, ROWS_W, 2 * RANK)
-    exchange = tuple(axis for axis in axes if axis != "rep")
+    exchange = (axes[-1],) + tuple(axis for axis in axes[:-1] if axis != "rep")
 
     def theirs(x):
         return lax.ppermute(x, "rep", [(0, 1), (1, 0)])

time: 53 us -> 51.7 us (0.975)
  waiting for transfers between devices: 5.48 us -> 3.62 us
    all_to_all x2, waiting for transfers between devices: 5.48 us -> 3.62 us  [on_device(): lax.all_to_all(sent, exchange, split_axis=0, concat_axis=0, tiled=True)]
  transfers between devices with their start and end apart: 3 -> 3, of which waited for: 2 -> 1; matrix products, arithmetic and copies ran while one was open for 0% -> 0% of each run, Pallas kernels for 45% -> 46%
where the time goes in v2:
time: 51.7 us; the launch traced here: 50.9 us
  Pallas kernels  30.1 us (58%)
  starting transfers between devices  14.1 us (27%)
  waiting for transfers between devices  3.62 us (7%)
  local copies, waits for them, and re-layouts  1.97 us (4%)
  other arithmetic  0.94 us (2%)
    pallas_call x4, Pallas kernels, call(): pl.pallas_call(functools.partial(kernel, bits, dev_bits), out_shape=out,...  30.1 us
    all_to_all x2, starting transfers between devices, on_device(): lax.all_to_all(sent, exchange, split_axis=0, concat_axis=0, tiled=True)  9.98 us
    ppermute x1, starting transfers between devices, theirs(): return lax.ppermute(x, 'rep', [(0, 1), (1, 0)])  4.11 us
    all_to_all x2, waiting for transfers between devices, on_device(): lax.all_to_all(sent, exchange, split_axis=0, concat_axis=0, tiled=True)  3.62 us
    unnamed x8, local copies, waits for them, and re-layouts  1.97 us
  transfers between devices with their start and end apart: 3, of which 1 were waited for; matrix products, arithmetic and copies ran while one was open for 0% of the time, Pallas kernels for 46%

profile of v2, /device:TPU:0, one launch (start us, length us, event | category | flops | bytes accessed | tf_op | source)
XLA Modules:
  0.0 50.9 jit_solution(8395479421744177264)
XLA Ops:
  0.0 0.9 %select_select_fusion = f32[32,1024]{1,0:T(8,128)S(1)} fusion(s32[13,256]{1,0:T(8,128)} %pat_hbm.1, f32[16,1024]{1,0:T(8,128)} %vals_hbm.1, s32[1024]{0:T(1024)} %param.9, f32[1024]{0:T(1024)} %param.8, pred[32]{0:T(512)(128)(4,1)S(1)} %get-tuple-element.13, pred[32]{0:T(512)(128)(4,1)S(1)} %get-tuple-element.14, pred[32]{0:T(512)(128)(4,1)S(1)} %iota_compare_fusion.2), kind=kLoop, calls=%fused_computation | loop fusion | flops 131072 | bytes 218208 | tf_op jit(solution)/shard_map/jit(_where)/select_n | solution.py:555
  0.9 4.1 %collective-permute-start = (f32[32,1024]{1,0:T(8,128)S(1)}, f32[32,1024]{1,0:T(8,128)S(1)}, u32[]{:S(2)}, u32[]{:S(2)}) collective-permute-start(f32[32,1024]{1,0:T(8,128)S(1)} %select_select_fusion), channel_id=1, source_target_pairs={{0,4},{4,0},{1,5},{5,1},{2,6},{6,2},{3,7},{7,3},{8,12},{12,8},{9,1... | collective-permute-start | bytes 393224 | tf_op jit(solution)/shard_map/ppermute | solution.py:513
  5.1 8.4 %own_half.1 = f32[16,72,128]{2,1,0:T(8,128)} custom-call(f32[16,1024]{1,0:T(8,128)} %vals_hbm.1, f32[1,1024]{1,0:T(1,128)} %bitcast.11, s32[1,1024]{1,0:T(1,128)} %bitcast.10, s32[13,256]{1,0:T(8,128)} %pat_hbm.1, f32[13,512,128]{2,1,0:T(8,128)} %bitcast.5), custom_call_target="tpu_custom_call" | custom-call | flops 5368709120 | bytes 4194304 | tf_op jit(solution)/shard_map/own_half/pallas_call | solution.py:522
  13.5 0.0 collective-permute-done.refs_0_
  13.5 0.0 copy-start.3
  13.5 4.9 %all-to-all-start.1 = ((f32[16,72,128]{2,1,0:T(8,128)}), f32[16,72,128]{2,1,0:T(8,128)S(1)}, u32[]{:S(2)}, u32[]{:S(2)}) async-start(f32[16,72,128]{2,1,0:T(8,128)} %own_half.1), calls=%async_computation.1 | async-start | bytes 1179648 | tf_op jit(solution)/shard_map/all_to_all | solution.py:567
  18.4 0.0 copy-done.3
  18.4 10.5 %partner_half.1 = f32[16,72,128]{2,1,0:T(8,128)} custom-call(f32[32,1024]{1,0:T(8,128)} %copy-done.3, f32[13,512,128]{2,1,0:T(8,128)} %bitcast.6), custom_call_target="tpu_custom_call" | custom-call | flops 8589934592 | bytes 4194304 | tf_op jit(solution)/shard_map/partner_half/pallas_call | solution.py:522
  28.9 0.0 all-to-all-done.1.refs_0_
  28.9 5.1 %all-to-all-start = ((f32[16,72,128]{2,1,0:T(8,128)}), f32[16,72,128]{2,1,0:T(8,128)S(1)}, u32[]{:S(2)}, u32[]{:S(2)}) async-start(f32[16,72,128]{2,1,0:T(8,128)} %partner_half.1), calls=%async_computation | async-start | bytes 1179648 | tf_op jit(solution)/shard_map/all_to_all | solution.py:577
  34.0 0.0 copy-start
  34.0 2.0 %copy-done = f32[13,4,2,64,128]{4,3,2,1,0:T(8,128)S(1)} copy-done((f32[13,4,2,64,128]{4,3,2,1,0:T(8,128)S(1)}, f32[13,4,2,64,128]{4,3,2,1,0:T(8,128)}, u32[]{:S(2)}) %copy-start) | copy-done | bytes 3407896
  36.0 0.0 copy-start.1
  36.0 0.0 copy-start.2
  36.0 4.3 %own_later.1 = (f32[1408,128]{1,0:T(8,128)S(1)}, bf16[5,256,512]{2,1,0:T(8,128)(2,1)S(1)}) custom-call(f32[16,72,128]{2,1,0:T(8,128)S(1)} %all-to-all-done.1.refs_0_, f32[13,512,128]{2,1,0:T(8,128)S(1)} %bitcast.7), custom_call_target="tpu_custom_call" | custom-call | flops 3221225472 | bytes 4194304 | tf_op jit(solution)/shard_map/own_later/pallas_call | solution.py:522
  40.3 3.6 %all-to-all-done.came = f32[16,72,128]{2,1,0:T(8,128)S(1)} async-done(((f32[16,72,128]{2,1,0:T(8,128)}), f32[16,72,128]{2,1,0:T(8,128)S(1)}, u32[]{:S(2)}, u32[]{:S(2)}) %all-to-all-start) | async-done | bytes 589856 | tf_op jit(solution)/shard_map/all_to_all | solution.py:577
  43.9 0.0 copy-done.1
  43.9 0.0 copy-done.2
  43.9 7.0 %join.1 = f32[16,1024]{1,0:T(8,128)} custom-call(f32[16,72,128]{2,1,0:T(8,128)S(1)} %all-to-all-done.came, f32[1408,128]{1,0:T(8,128)S(1)} %get-tuple-element.11.own, bf16[5,256,512]{2,1,0:T(8,128)(2,1)S(1)} %get-tuple-element.12.weights, f32[1,1024]{1,0:T(1,128)S(1)} %bitcast.8, s32[1,1024]{1,0:T(1,128)S(1)} %bitcast.9), custom_call_target="tpu_custom_call" | custom-call | flops 5368709120 | bytes 4194304 | tf_op jit(solution)/shard_map/join/pallas_call | solution.py:522
  (2 shorter events, 0.0 us)
Async XLA Ops:
  0.9 12.6 %collective-permute-start = (f32[32,1024]{1,0:T(8,128)S(1)}, f32[32,1024]{1,0:T(8,128)S(1)}, u32[]{:S(2)}, u32[]{:S(2)}) collective-permute-start(f32[32,1024]{1,0:T(8,128)S(1)} %select_select_fusion), channel_id=1, source_target_pairs={{0,4},{4,0},{1,5},{5,1},{2,6},{6,2},{3,7},{7,3},{8,12},{12,8},{9,1... | collective-permute-start | bytes 393224 | tf_op jit(solution)/shard_map/ppermute | solution.py:513
  13.5 4.9 %copy-start.3 = (f32[32,1024]{1,0:T(8,128)}, f32[32,1024]{1,0:T(8,128)S(1)}, u32[]{:S(2)}) copy-start(f32[32,1024]{1,0:T(8,128)S(1)} %collective-permute-done.refs_0_) | copy-start | bytes 393220
  13.5 15.4 %all-to-all-start.1 = ((f32[16,72,128]{2,1,0:T(8,128)}), f32[16,72,128]{2,1,0:T(8,128)S(1)}, u32[]{:S(2)}, u32[]{:S(2)}) async-start(f32[16,72,128]{2,1,0:T(8,128)} %own_half.1), calls=%async_computation.1 | async-start | bytes 1179648 | tf_op jit(solution)/shard_map/all_to_all | solution.py:567
  28.9 15.0 %all-to-all-start = ((f32[16,72,128]{2,1,0:T(8,128)}), f32[16,72,128]{2,1,0:T(8,128)S(1)}, u32[]{:S(2)}, u32[]{:S(2)}) async-start(f32[16,72,128]{2,1,0:T(8,128)} %partner_half.1), calls=%async_computation | async-start | bytes 1179648 | tf_op jit(solution)/shard_map/all_to_all | solution.py:577
  34.0 2.0 %copy-start = (f32[13,4,2,64,128]{4,3,2,1,0:T(8,128)S(1)}, f32[13,4,2,64,128]{4,3,2,1,0:T(8,128)}, u32[]{:S(2)}) copy-start(f32[13,4,2,64,128]{4,3,2,1,0:T(8,128)} %param.13) | copy-start | bytes 10223620
  36.0 7.9 %copy-start.1 = (f32[1024]{0:T(1024)S(1)}, f32[1024]{0:T(1024)}, u32[]{:S(2)}) copy-start(f32[1024]{0:T(1024)} %param.10) | copy-start | bytes 12292
  36.0 7.9 %copy-start.2 = (s32[1024]{0:T(1024)S(1)}, s32[1024]{0:T(1024)}, u32[]{:S(2)}) copy-start(s32[1024]{0:T(1024)} %param.11) | copy-start | bytes 12292

commit v3 on v2

--- a/solution.py
+++ b/solution.py
@@ -50,7 +50,13 @@
 
 
 def slot(group, dev_bits):
-    return rotate_right(group, REP, dev_bits - 1)
+    near = rotate_right(group & ((1 << REP) - 1), 1, REP)
+    return (near << (dev_bits - 1 - REP)) | (group >> REP)
+
+
+def group_at(slot, dev_bits):
+    rest = dev_bits - 1 - REP
+    return ((slot & ((1 << rest) - 1)) << REP) | rotate_left(slot >> rest, 1, REP)
 
 
 def remove(x, bit):
@@ -368,7 +374,7 @@
     if nbits < bits:
         at = insert(at, dev_bits - 1 - REP, half)
     column = iota((1, table.shape[0]), 1)
-    device = reverse(insert(rotate_left(column >> 3, REP, dev_bits - 1), REP, half), dev_bits)
+    device = reverse(insert(group_at(column >> 3, dev_bits), REP, half), dev_bits)
     lane = iota((1, LANES), 1)
     lane_key = jnp.where(lane < (1 << upper), reverse(lane, upper), -1)
     low = jnp.concatenate([at & ((1 << dev_bits) - 1)] * (table.shape[0] // LANES), axis=1)
@@ -507,7 +513,7 @@
     rows = pairs * funcs
     each = rows // 2 // groups
     ops = operators.reshape(levels, ROWS_W, 2 * RANK)
-    exchange = (axes[-1],) + tuple(axis for axis in axes[:-1] if axis != "rep")
+    exchange = ("core", "mid", "src", "far")
 
     def theirs(x):
         return lax.ppermute(x, "rep", [(0, 1), (1, 0)])
@@ -600,8 +606,8 @@
 
 def solution(mesh):
     src, tgt = mesh.shape["src"], mesh.shape["tgt"]
-    axes = ("src", "far", "rep", "near")
-    devices = mesh.devices.reshape(src, tgt >> (REP + 1), 2, 1 << REP)
+    axes = ("src", "far", "rep", "mid", "core")
+    devices = mesh.devices.reshape(src, tgt >> (REP + 1), 2, 1 << (REP - 1), 2)
     placed = (P(None, axes), P(axes), P(axes), P(axes), P(axes), P(None, axes), P())
     return jax.shard_map(
         functools.partial(on_device, axes),

time: 51.7 us -> 51.7 us (level)
  transfers between devices with their start and end apart: 3 -> 3, of which waited for: 1 -> 1; matrix products, arithmetic and copies ran while one was open for 0% -> 0% of each run, Pallas kernels for 46% -> 45%
where the time goes in v3:
time: 51.7 us; the launch traced here: 51.2 us
  Pallas kernels  30.1 us (58%)
  starting transfers between devices  14.1 us (27%)
  waiting for transfers between devices  3.97 us (8%)
  local copies, waits for them, and re-layouts  1.97 us (4%)
  other arithmetic  0.94 us (2%)
    pallas_call x4, Pallas kernels, call(): pl.pallas_call(functools.partial(kernel, bits, dev_bits), out_shape=out,...  30.1 us
    all_to_all x2, starting transfers between devices, on_device(): lax.all_to_all(sent, exchange, split_axis=0, concat_axis=0, tiled=True)  9.98 us
    ppermute x1, starting transfers between devices, theirs(): return lax.ppermute(x, 'rep', [(0, 1), (1, 0)])  4.11 us
    all_to_all x2, waiting for transfers between devices, on_device(): lax.all_to_all(sent, exchange, split_axis=0, concat_axis=0, tiled=True)  3.97 us
    unnamed x8, local copies, waits for them, and re-layouts  1.97 us
  transfers between devices with their start and end apart: 3, of which 1 were waited for; matrix products, arithmetic and copies ran while one was open for 0% of the time, Pallas kernels for 45%

profile of v3, /device:TPU:0, one launch (start us, length us, event | category | flops | bytes accessed | tf_op | source)
XLA Modules:
  0.0 51.2 jit_solution(11280778376164230649)
XLA Ops:
  0.0 0.9 %select_select_fusion = f32[32,1024]{1,0:T(8,128)S(1)} fusion(s32[13,256]{1,0:T(8,128)} %pat_hbm.1, f32[16,1024]{1,0:T(8,128)} %vals_hbm.1, s32[1024]{0:T(1024)} %param.9, f32[1024]{0:T(1024)} %param.8, pred[32]{0:T(512)(128)(4,1)S(1)} %get-tuple-element.13, pred[32]{0:T(512)(128)(4,1)S(1)} %get-tuple-element.14, pred[32]{0:T(512)(128)(4,1)S(1)} %iota_compare_fusion.2), kind=kLoop, calls=%fused_computation | loop fusion | flops 131072 | bytes 218208 | tf_op jit(solution)/shard_map/jit(_where)/select_n | solution.py:561
  0.9 4.1 %collective-permute-start = (f32[32,1024]{1,0:T(8,128)S(1)}, f32[32,1024]{1,0:T(8,128)S(1)}, u32[]{:S(2)}, u32[]{:S(2)}) collective-permute-start(f32[32,1024]{1,0:T(8,128)S(1)} %select_select_fusion), channel_id=1, source_target_pairs={{0,4},{4,0},{1,5},{5,1},{2,6},{6,2},{3,7},{7,3},{8,12},{12,8},{9,1... | collective-permute-start | bytes 393224 | tf_op jit(solution)/shard_map/ppermute | solution.py:519
  5.1 8.4 %own_half.1 = f32[16,72,128]{2,1,0:T(8,128)} custom-call(f32[16,1024]{1,0:T(8,128)} %vals_hbm.1, f32[1,1024]{1,0:T(1,128)} %bitcast.11, s32[1,1024]{1,0:T(1,128)} %bitcast.10, s32[13,256]{1,0:T(8,128)} %pat_hbm.1, f32[13,512,128]{2,1,0:T(8,128)} %bitcast.5), custom_call_target="tpu_custom_call" | custom-call | flops 5368709120 | bytes 4194304 | tf_op jit(solution)/shard_map/own_half/pallas_call | solution.py:528
  13.5 0.0 collective-permute-done.refs_0_
  13.5 0.0 copy-start.3
  13.5 4.9 %all-to-all-start.1 = ((f32[16,72,128]{2,1,0:T(8,128)}), f32[16,72,128]{2,1,0:T(8,128)S(1)}, u32[]{:S(2)}, u32[]{:S(2)}) async-start(f32[16,72,128]{2,1,0:T(8,128)} %own_half.1), calls=%async_computation.1 | async-start | bytes 1179648 | tf_op jit(solution)/shard_map/all_to_all | solution.py:573
  18.4 0.0 copy-done.3
  18.4 10.5 %partner_half.1 = f32[16,72,128]{2,1,0:T(8,128)} custom-call(f32[32,1024]{1,0:T(8,128)} %copy-done.3, f32[13,512,128]{2,1,0:T(8,128)} %bitcast.6), custom_call_target="tpu_custom_call" | custom-call | flops 8589934592 | bytes 4194304 | tf_op jit(solution)/shard_map/partner_half/pallas_call | solution.py:528
  28.9 0.0 all-to-all-done.1.refs_0_
  28.9 5.1 %all-to-all-start = ((f32[16,72,128]{2,1,0:T(8,128)}), f32[16,72,128]{2,1,0:T(8,128)S(1)}, u32[]{:S(2)}, u32[]{:S(2)}) async-start(f32[16,72,128]{2,1,0:T(8,128)} %partner_half.1), calls=%async_computation | async-start | bytes 1179648 | tf_op jit(solution)/shard_map/all_to_all | solution.py:583
  34.0 0.0 copy-start
  34.0 2.0 %copy-done = f32[13,4,2,64,128]{4,3,2,1,0:T(8,128)S(1)} copy-done((f32[13,4,2,64,128]{4,3,2,1,0:T(8,128)S(1)}, f32[13,4,2,64,128]{4,3,2,1,0:T(8,128)}, u32[]{:S(2)}) %copy-start) | copy-done | bytes 3407896
  36.0 0.0 copy-start.1
  36.0 0.0 copy-start.2
  36.0 4.3 %own_later.1 = (f32[1408,128]{1,0:T(8,128)S(1)}, bf16[5,256,512]{2,1,0:T(8,128)(2,1)S(1)}) custom-call(f32[16,72,128]{2,1,0:T(8,128)S(1)} %all-to-all-done.1.refs_0_, f32[13,512,128]{2,1,0:T(8,128)S(1)} %bitcast.7), custom_call_target="tpu_custom_call" | custom-call | flops 3221225472 | bytes 4194304 | tf_op jit(solution)/shard_map/own_later/pallas_call | solution.py:528
  40.3 4.0 %all-to-all-done.came = f32[16,72,128]{2,1,0:T(8,128)S(1)} async-done(((f32[16,72,128]{2,1,0:T(8,128)}), f32[16,72,128]{2,1,0:T(8,128)S(1)}, u32[]{:S(2)}, u32[]{:S(2)}) %all-to-all-start) | async-done | bytes 589856 | tf_op jit(solution)/shard_map/all_to_all | solution.py:583
  44.3 0.0 copy-done.1
  44.3 0.0 copy-done.2
  44.3 6.9 %join.1 = f32[16,1024]{1,0:T(8,128)} custom-call(f32[16,72,128]{2,1,0:T(8,128)S(1)} %all-to-all-done.came, f32[1408,128]{1,0:T(8,128)S(1)} %get-tuple-element.11.own, bf16[5,256,512]{2,1,0:T(8,128)(2,1)S(1)} %get-tuple-element.12.weights, f32[1,1024]{1,0:T(1,128)S(1)} %bitcast.8, s32[1,1024]{1,0:T(1,128)S(1)} %bitcast.9), custom_call_target="tpu_custom_call" | custom-call | flops 5368709120 | bytes 4194304 | tf_op jit(solution)/shard_map/join/pallas_call | solution.py:528
  (2 shorter events, 0.0 us)
Async XLA Ops:
  0.9 12.6 %collective-permute-start = (f32[32,1024]{1,0:T(8,128)S(1)}, f32[32,1024]{1,0:T(8,128)S(1)}, u32[]{:S(2)}, u32[]{:S(2)}) collective-permute-start(f32[32,1024]{1,0:T(8,128)S(1)} %select_select_fusion), channel_id=1, source_target_pairs={{0,4},{4,0},{1,5},{5,1},{2,6},{6,2},{3,7},{7,3},{8,12},{12,8},{9,1... | collective-permute-start | bytes 393224 | tf_op jit(solution)/shard_map/ppermute | solution.py:519
  13.5 4.9 %copy-start.3 = (f32[32,1024]{1,0:T(8,128)}, f32[32,1024]{1,0:T(8,128)S(1)}, u32[]{:S(2)}) copy-start(f32[32,1024]{1,0:T(8,128)S(1)} %collective-permute-done.refs_0_) | copy-start | bytes 393220
  13.5 15.4 %all-to-all-start.1 = ((f32[16,72,128]{2,1,0:T(8,128)}), f32[16,72,128]{2,1,0:T(8,128)S(1)}, u32[]{:S(2)}, u32[]{:S(2)}) async-start(f32[16,72,128]{2,1,0:T(8,128)} %own_half.1), calls=%async_computation.1 | async-start | bytes 1179648 | tf_op jit(solution)/shard_map/all_to_all | solution.py:573
  28.9 15.3 %all-to-all-start = ((f32[16,72,128]{2,1,0:T(8,128)}), f32[16,72,128]{2,1,0:T(8,128)S(1)}, u32[]{:S(2)}, u32[]{:S(2)}) async-start(f32[16,72,128]{2,1,0:T(8,128)} %partner_half.1), calls=%async_computation | async-start | bytes 1179648 | tf_op jit(solution)/shard_map/all_to_all | solution.py:583
  34.0 2.0 %copy-start = (f32[13,4,2,64,128]{4,3,2,1,0:T(8,128)S(1)}, f32[13,4,2,64,128]{4,3,2,1,0:T(8,128)}, u32[]{:S(2)}) copy-start(f32[13,4,2,64,128]{4,3,2,1,0:T(8,128)} %param.13) | copy-start | bytes 10223620
  36.0 8.3 %copy-start.1 = (f32[1024]{0:T(1024)S(1)}, f32[1024]{0:T(1024)}, u32[]{:S(2)}) copy-start(f32[1024]{0:T(1024)} %param.10) | copy-start | bytes 12292
  36.0 8.3 %copy-start.2 = (s32[1024]{0:T(1024)S(1)}, s32[1024]{0:T(1024)}, u32[]{:S(2)}) copy-start(s32[1024]{0:T(1024)} %param.11) | copy-start | bytes 12292

commit v4 on v3

--- a/solution.py
+++ b/solution.py
@@ -50,13 +50,13 @@
 
 
 def slot(group, dev_bits):
-    near = rotate_right(group & ((1 << REP) - 1), 1, REP)
-    return (near << (dev_bits - 1 - REP)) | (group >> REP)
+    near, rest = group & ((1 << REP) - 1), group >> REP
+    return ((near & 1) << (dev_bits - 2)) | (rest << (REP - 1)) | (near >> 1)
 
 
 def group_at(slot, dev_bits):
-    rest = dev_bits - 1 - REP
-    return ((slot & ((1 << rest) - 1)) << REP) | rotate_left(slot >> rest, 1, REP)
+    rest = (slot & ((1 << (dev_bits - 2)) - 1)) >> (REP - 1)
+    return (rest << REP) | ((slot & ((1 << (REP - 1)) - 1)) << 1) | (slot >> (dev_bits - 2))
 
 
 def remove(x, bit):
@@ -513,7 +513,7 @@
     rows = pairs * funcs
     each = rows // 2 // groups
     ops = operators.reshape(levels, ROWS_W, 2 * RANK)
-    exchange = ("core", "mid", "src", "far")
+    exchange = ("core", "src", "far", "mid")
 
     def theirs(x):
         return lax.ppermute(x, "rep", [(0, 1), (1, 0)])

time: 51.7 us -> 51.4 us (level)
  transfers between devices with their start and end apart: 3 -> 3, of which waited for: 1 -> 1; matrix products, arithmetic and copies ran while one was open for 0% -> 0% of each run, Pallas kernels for 45% -> 46%
where the time goes in v4:
time: 51.4 us; the launch traced here: 50.9 us
  Pallas kernels  30.1 us (59%)
  starting transfers between devices  14.1 us (27%)
  waiting for transfers between devices  3.7 us (7%)
  local copies, waits for them, and re-layouts  1.97 us (4%)
  other arithmetic  0.94 us (2%)
    pallas_call x4, Pallas kernels, call(): pl.pallas_call(functools.partial(kernel, bits, dev_bits), out_shape=out,...  30.1 us
    all_to_all x2, starting transfers between devices, on_device(): lax.all_to_all(sent, exchange, split_axis=0, concat_axis=0, tiled=True)  9.98 us
    ppermute x1, starting transfers between devices, theirs(): return lax.ppermute(x, 'rep', [(0, 1), (1, 0)])  4.11 us
    all_to_all x2, waiting for transfers between devices, on_device(): lax.all_to_all(sent, exchange, split_axis=0, concat_axis=0, tiled=True)  3.7 us
    unnamed x8, local copies, waits for them, and re-layouts  1.97 us
  transfers between devices with their start and end apart: 3, of which 1 were waited for; matrix products, arithmetic and copies ran while one was open for 0% of the time, Pallas kernels for 46%

profile of v4, /device:TPU:0, one launch (start us, length us, event | category | flops | bytes accessed | tf_op | source)
XLA Modules:
  0.0 50.9 jit_solution(5809798727684800569)
XLA Ops:
  0.0 0.9 %select_select_fusion = f32[32,1024]{1,0:T(8,128)S(1)} fusion(s32[13,256]{1,0:T(8,128)} %pat_hbm.1, f32[16,1024]{1,0:T(8,128)} %vals_hbm.1, s32[1024]{0:T(1024)} %param.9, f32[1024]{0:T(1024)} %param.8, pred[32]{0:T(512)(128)(4,1)S(1)} %get-tuple-element.13, pred[32]{0:T(512)(128)(4,1)S(1)} %get-tuple-element.14, pred[32]{0:T(512)(128)(4,1)S(1)} %iota_compare_fusion.2), kind=kLoop, calls=%fused_computation | loop fusion | flops 131072 | bytes 218208 | tf_op jit(solution)/shard_map/jit(_where)/select_n | solution.py:561
  0.9 4.1 %collective-permute-start = (f32[32,1024]{1,0:T(8,128)S(1)}, f32[32,1024]{1,0:T(8,128)S(1)}, u32[]{:S(2)}, u32[]{:S(2)}) collective-permute-start(f32[32,1024]{1,0:T(8,128)S(1)} %select_select_fusion), channel_id=1, source_target_pairs={{0,4},{4,0},{1,5},{5,1},{2,6},{6,2},{3,7},{7,3},{8,12},{12,8},{9,1... | collective-permute-start | bytes 393224 | tf_op jit(solution)/shard_map/ppermute | solution.py:519
  5.1 8.4 %own_half.1 = f32[16,72,128]{2,1,0:T(8,128)} custom-call(f32[16,1024]{1,0:T(8,128)} %vals_hbm.1, f32[1,1024]{1,0:T(1,128)} %bitcast.11, s32[1,1024]{1,0:T(1,128)} %bitcast.10, s32[13,256]{1,0:T(8,128)} %pat_hbm.1, f32[13,512,128]{2,1,0:T(8,128)} %bitcast.5), custom_call_target="tpu_custom_call" | custom-call | flops 5368709120 | bytes 4194304 | tf_op jit(solution)/shard_map/own_half/pallas_call | solution.py:528
  13.5 0.0 collective-permute-done.refs_0_
  13.5 0.0 copy-start.3
  13.5 4.9 %all-to-all-start.1 = ((f32[16,72,128]{2,1,0:T(8,128)}), f32[16,72,128]{2,1,0:T(8,128)S(1)}, u32[]{:S(2)}, u32[]{:S(2)}) async-start(f32[16,72,128]{2,1,0:T(8,128)} %own_half.1), calls=%async_computation.1 | async-start | bytes 1179648 | tf_op jit(solution)/shard_map/all_to_all | solution.py:573
  18.4 0.0 copy-done.3
  18.4 10.5 %partner_half.1 = f32[16,72,128]{2,1,0:T(8,128)} custom-call(f32[32,1024]{1,0:T(8,128)} %copy-done.3, f32[13,512,128]{2,1,0:T(8,128)} %bitcast.6), custom_call_target="tpu_custom_call" | custom-call | flops 8589934592 | bytes 4194304 | tf_op jit(solution)/shard_map/partner_half/pallas_call | solution.py:528
  28.9 0.0 all-to-all-done.1.refs_0_
  28.9 5.1 %all-to-all-start = ((f32[16,72,128]{2,1,0:T(8,128)}), f32[16,72,128]{2,1,0:T(8,128)S(1)}, u32[]{:S(2)}, u32[]{:S(2)}) async-start(f32[16,72,128]{2,1,0:T(8,128)} %partner_half.1), calls=%async_computation | async-start | bytes 1179648 | tf_op jit(solution)/shard_map/all_to_all | solution.py:583
  34.0 0.0 copy-start
  34.0 2.0 %copy-done = f32[13,4,2,64,128]{4,3,2,1,0:T(8,128)S(1)} copy-done((f32[13,4,2,64,128]{4,3,2,1,0:T(8,128)S(1)}, f32[13,4,2,64,128]{4,3,2,1,0:T(8,128)}, u32[]{:S(2)}) %copy-start) | copy-done | bytes 3407896
  36.0 0.0 copy-start.1
  36.0 0.0 copy-start.2
  36.0 4.3 %own_later.1 = (f32[1408,128]{1,0:T(8,128)S(1)}, bf16[5,256,512]{2,1,0:T(8,128)(2,1)S(1)}) custom-call(f32[16,72,128]{2,1,0:T(8,128)S(1)} %all-to-all-done.1.refs_0_, f32[13,512,128]{2,1,0:T(8,128)S(1)} %bitcast.7), custom_call_target="tpu_custom_call" | custom-call | flops 3221225472 | bytes 4194304 | tf_op jit(solution)/shard_map/own_later/pallas_call | solution.py:528
  40.3 3.7 %all-to-all-done.came = f32[16,72,128]{2,1,0:T(8,128)S(1)} async-done(((f32[16,72,128]{2,1,0:T(8,128)}), f32[16,72,128]{2,1,0:T(8,128)S(1)}, u32[]{:S(2)}, u32[]{:S(2)}) %all-to-all-start) | async-done | bytes 589856 | tf_op jit(solution)/shard_map/all_to_all | solution.py:583
  44.0 0.0 copy-done.1
  44.0 0.0 copy-done.2
  44.0 6.9 %join.1 = f32[16,1024]{1,0:T(8,128)} custom-call(f32[16,72,128]{2,1,0:T(8,128)S(1)} %all-to-all-done.came, f32[1408,128]{1,0:T(8,128)S(1)} %get-tuple-element.11.own, bf16[5,256,512]{2,1,0:T(8,128)(2,1)S(1)} %get-tuple-element.12.weights, f32[1,1024]{1,0:T(1,128)S(1)} %bitcast.8, s32[1,1024]{1,0:T(1,128)S(1)} %bitcast.9), custom_call_target="tpu_custom_call" | custom-call | flops 5368709120 | bytes 4194304 | tf_op jit(solution)/shard_map/join/pallas_call | solution.py:528
  (2 shorter events, 0.0 us)
Async XLA Ops:
  0.9 12.6 %collective-permute-start = (f32[32,1024]{1,0:T(8,128)S(1)}, f32[32,1024]{1,0:T(8,128)S(1)}, u32[]{:S(2)}, u32[]{:S(2)}) collective-permute-start(f32[32,1024]{1,0:T(8,128)S(1)} %select_select_fusion), channel_id=1, source_target_pairs={{0,4},{4,0},{1,5},{5,1},{2,6},{6,2},{3,7},{7,3},{8,12},{12,8},{9,1... | collective-permute-start | bytes 393224 | tf_op jit(solution)/shard_map/ppermute | solution.py:519
  13.5 4.9 %copy-start.3 = (f32[32,1024]{1,0:T(8,128)}, f32[32,1024]{1,0:T(8,128)S(1)}, u32[]{:S(2)}) copy-start(f32[32,1024]{1,0:T(8,128)S(1)} %collective-permute-done.refs_0_) | copy-start | bytes 393220
  13.5 15.4 %all-to-all-start.1 = ((f32[16,72,128]{2,1,0:T(8,128)}), f32[16,72,128]{2,1,0:T(8,128)S(1)}, u32[]{:S(2)}, u32[]{:S(2)}) async-start(f32[16,72,128]{2,1,0:T(8,128)} %own_half.1), calls=%async_computation.1 | async-start | bytes 1179648 | tf_op jit(solution)/shard_map/all_to_all | solution.py:573
  28.9 15.1 %all-to-all-start = ((f32[16,72,128]{2,1,0:T(8,128)}), f32[16,72,128]{2,1,0:T(8,128)S(1)}, u32[]{:S(2)}, u32[]{:S(2)}) async-start(f32[16,72,128]{2,1,0:T(8,128)} %partner_half.1), calls=%async_computation | async-start | bytes 1179648 | tf_op jit(solution)/shard_map/all_to_all | solution.py:583
  34.0 2.0 %copy-start = (f32[13,4,2,64,128]{4,3,2,1,0:T(8,128)S(1)}, f32[13,4,2,64,128]{4,3,2,1,0:T(8,128)}, u32[]{:S(2)}) copy-start(f32[13,4,2,64,128]{4,3,2,1,0:T(8,128)} %param.13) | copy-start | bytes 10223620
  36.0 8.0 %copy-start.1 = (f32[1024]{0:T(1024)S(1)}, f32[1024]{0:T(1024)}, u32[]{:S(2)}) copy-start(f32[1024]{0:T(1024)} %param.10) | copy-start | bytes 12292
  36.0 8.0 %copy-start.2 = (s32[1024]{0:T(1024)S(1)}, s32[1024]{0:T(1024)}, u32[]{:S(2)}) copy-start(s32[1024]{0:T(1024)} %param.11) | copy-start | bytes 12292
